TPU v7x, 32 devices: a whole 2x2x4 slice. The times are simulated.
32 devices in a mesh: row: 2 (over core), col: 16 (over z, y, x).
Axes of the slice: x: 2, y: 2, z: 4, core: 2. Of those that a mesh axis runs over, the one named last changes fastest.
Arguments:
- pair_activations: bfloat16 [1024, 1024, 128], P('row', 'col'), may hold values from -40 to 40
- pair_logit_weight: bfloat16 [128, 8], replicated, may hold values from -0.7 to 0.7
- normed_strand_features: bfloat16 [256, 1024, 64], P('row', 'col'), may hold values from -6 to 6
- mean_output_sensitivity: bfloat16 [256, 1024, 64], P('col', 'row'), may hold values from -96 to 96
- projected_entries: bfloat16 [64, 64], replicated, may hold values from -0.75 to 0.75
Outputs:
- d_pair: bfloat16 [1024, 1024, 128], P('row', 'col')
- grad_pair_weight: float32 [128, 8], replicated
- value_weight_gradient: float32 [64, 64], replicated
All inputs are finite; a program needn't handle non-finite values.
Results may differ from a plain program's by a relative error of at most 0.018.
Values may be sent and summed in bfloat16 or wider, within the bound.
A program may use at most 128 MiB of HBM per device.

v0:
```python
import functools
import math

import jax
import jax.numpy as jnp
from jax import lax
from jax.experimental import pallas as pl
from jax.experimental.pallas import tpu as pltpu
from jax.sharding import PartitionSpec as P

MESH = pl.DeviceIdType.MESH
VMEM_BYTES = 48 * 1024 * 1024


def exchange_kernel(axes, combine, mine, out, slots, send, recv):
    sizes = [lax.axis_size(a) for a in axes]
    n = math.prod(sizes)
    me = lax.axis_index(axes[0])
    for a, size in zip(axes[1:], sizes[1:]):
        me = me * size + lax.axis_index(a)

    def device(p):
        if len(axes) == 1:
            return {axes[0]: p}
        return {axes[0]: p // sizes[1], axes[1]: p % sizes[1]}

    barrier = pltpu.get_barrier_semaphore()

    def greet(d, carry):
        pl.semaphore_signal(barrier, inc=1, device_id=device(lax.rem(me + d, n)), device_id_type=MESH)
        return carry

    lax.fori_loop(1, n, greet, 0)
    pl.semaphore_wait(barrier, n - 1)

    def copy(to, slot):
        return pltpu.make_async_remote_copy(
            src_ref=mine, dst_ref=slots.at[slot], send_sem=send.at[to], recv_sem=recv.at[slot],
            device_id=device(to), device_id_type=MESH)

    def begin(d, carry):
        copy(lax.rem(me + d, n), me).start()
        return carry

    lax.fori_loop(1, n, begin, 0)
    slots[me] = mine[...]

    def finish(d, carry):
        peer = lax.rem(me + d, n)
        copy(peer, peer).wait_recv()
        copy(peer, me).wait_send()
        return carry

    lax.fori_loop(1, n, finish, 0)
    combine(n, slots, out)


def add_up(n, slots, out):
    out[...] = lax.fori_loop(1, n, lambda p, total: total + slots[p], slots[0])


def join_softmax(n, slots, out):
    top = lax.fori_loop(1, n, lambda p, m: jnp.maximum(m, slots[p, 0]), slots[0, 0])
    total = lax.fori_loop(
        0, n, lambda p, t: t + slots[p, 1] * jnp.exp(slots[p, 0] - top), jnp.zeros_like(top))
    out[0] = top
    out[1] = total


def exchange(x, axes, combine, collective_id):
    n = math.prod(lax.axis_size(a) for a in axes)
    return pl.pallas_call(
        functools.partial(exchange_kernel, axes, combine),
        out_shape=jax.ShapeDtypeStruct(x.shape, x.dtype),
        in_specs=[pl.BlockSpec(memory_space=pltpu.VMEM)],
        out_specs=pl.BlockSpec(memory_space=pltpu.VMEM),
        scratch_shapes=[
            pltpu.VMEM((n,) + x.shape, x.dtype),
            pltpu.SemaphoreType.DMA((n,)),
            pltpu.SemaphoreType.DMA((n,)),
        ],
        compiler_params=pltpu.CompilerParams(
            collective_id=collective_id, has_side_effects=True, vmem_limit_bytes=VMEM_BYTES),
    )(x)


def d_probs_kernel(heads, own, g, v, d_own, d_other, total):
    step = pl.program_id(0)

    @pl.when(step == 0)
    def _():
        total[...] = jnp.zeros_like(total)

    for h in range(heads):
        total[h] += lax.dot_general(
            v[h], g[0, h], (((1,), (1,)), ((), ())), preferred_element_type=jnp.float32)

    @pl.when(step == pl.num_programs(0) - 1)
    def _():
        d_own[...] = total[:, :own]
        d_other[...] = total[:, own:].astype(jnp.bfloat16)


def whole(shape):
    return pl.BlockSpec(shape, lambda c: (0,) * len(shape))


def d_probs_of(g, v):
    steps, heads, rows, lanes = g.shape
    tokens = v.shape[1]
    half = (heads, tokens // 2, rows)
    return pl.pallas_call(
        functools.partial(d_probs_kernel, heads, tokens // 2),
        grid=(steps,),
        in_specs=[
            pl.BlockSpec((1, heads, rows, lanes), lambda c: (c, 0, 0, 0)),
            pl.BlockSpec((heads, tokens, lanes), lambda c: (0, 0, c)),
        ],
        out_specs=[whole(half), whole(half)],
        out_shape=[jax.ShapeDtypeStruct(half, jnp.float32), jax.ShapeDtypeStruct(half, jnp.bfloat16)],
        scratch_shapes=[pltpu.VMEM((heads, tokens, rows), jnp.float32)],
        compiler_params=pltpu.CompilerParams(vmem_limit_bytes=VMEM_BYTES),
        cost_estimate=pl.CostEstimate(
            flops=2 * g.size * tokens, bytes_accessed=2 * g.size, transcendentals=0),
    )(g, v)


def value_kernel(heads, strands, g, p, f, weight, d_values):
    step = pl.program_id(0)
    tokens, lanes = p.shape[1], g.shape[3]
    rows = pl.ds(pl.multiple_of(step * tokens, tokens), tokens)
    for h in range(heads):
        d_values[rows, h * lanes:(h + 1) * lanes] = jnp.dot(
            p[h], g[0, h], preferred_element_type=jnp.float32).astype(jnp.bfloat16)

    @pl.when(step == pl.num_programs(0) - 1)
    def _():
        width = f.shape[0] // strands
        head_width = lanes // strands
        strand_of_lane = (lax.broadcasted_iota(jnp.int32, (width, heads * lanes), 1) % lanes) // head_width
        part = strands // 4
        total = jnp.zeros((width, heads * lanes), jnp.float32)
        for q in range(4):
            cross = jnp.dot(
                f[q * part * width:(q + 1) * part * width, :], d_values[...],
                preferred_element_type=jnp.float32)
            for s in range(part):
                total += jnp.where(
                    strand_of_lane == q * part + s, cross[s * width:(s + 1) * width], 0.0)
        weight[...] = total


def value_weight_of(g, p, f, strands):
    steps, heads, rows, lanes = g.shape
    tokens = p.shape[1]
    width = f.shape[0] // strands
    return pl.pallas_call(
        functools.partial(value_kernel, heads, strands),
        grid=(steps,),
        in_specs=[
            pl.BlockSpec((1, heads, rows, lanes), lambda c: (c, 0, 0, 0)),
            whole(p.shape),
            whole(f.shape),
        ],
        out_specs=whole((width, heads * lanes)),
        out_shape=jax.ShapeDtypeStruct((width, heads * lanes), jnp.float32),
        scratch_shapes=[pltpu.VMEM((steps * tokens, heads * lanes), jnp.bfloat16)],
        compiler_params=pltpu.CompilerParams(vmem_limit_bytes=VMEM_BYTES),
        cost_estimate=pl.CostEstimate(
            flops=4 * g.size * tokens, bytes_accessed=2 * g.size, transcendentals=0),
    )(g, p, f)


def pair_kernel(d_logits, pair, weight, d_pair, d_weight):
    @pl.when(pl.program_id(0) == 0)
    def _():
        d_weight[...] = jnp.zeros_like(d_weight)

    d_pair[...] = lax.dot_general(
        d_logits[...], weight[...], (((0,), (0,)), ((), ())), preferred_element_type=jnp.float32
    ).astype(jnp.bfloat16)
    d_weight[...] += jnp.dot(d_logits[...], pair[...], preferred_element_type=jnp.float32)


def pair_gradients(d_logits, pair, weight):
    heads, cells = d_logits.shape
    width = pair.shape[1]
    block = 4096
    return pl.pallas_call(
        pair_kernel,
        grid=(cells // block,),
        in_specs=[
            pl.BlockSpec((heads, block), lambda c: (0, c)),
            pl.BlockSpec((block, width), lambda c: (c, 0)),
            whole((heads, width)),
        ],
        out_specs=[pl.BlockSpec((block, width), lambda c: (c, 0)), whole((heads, width))],
        out_shape=[
            jax.ShapeDtypeStruct((cells, width), jnp.bfloat16),
            jax.ShapeDtypeStruct((heads, width), jnp.float32),
        ],
        compiler_params=pltpu.CompilerParams(vmem_limit_bytes=VMEM_BYTES),
    )(d_logits, pair, weight)


def on_device(pair, pair_weight, features, sensitivity, entries):
    rows, tokens, pair_width = pair.shape
    heads = pair_weight.shape[1]
    strands, _, width = sensitivity.shape
    head_width = width // heads
    blocks = lax.axis_size("col")
    token_total = tokens * blocks
    lanes = strands * head_width
    parity = lax.axis_index("col") % 2
    groups = [list(range(q, blocks, 2)) for q in range(2)]
    partners = [(c, c ^ 1) for c in range(blocks)]

    features = features.reshape(-1, 2, strands, tokens, width)
    kept = lax.dynamic_index_in_dim(features, parity, 1, keepdims=False)
    sent = lax.dynamic_index_in_dim(features, 1 - parity, 1, keepdims=False)
    both_tokens = jnp.concatenate([kept, lax.ppermute(sent, "col", partners)], axis=2)

    g = sensitivity.reshape(strands, rows, heads, head_width)
    g = g.transpose(2, 1, 0, 3).reshape(heads, rows, lanes)
    g = lax.all_gather(g, "col", axis=0, axis_index_groups=groups)

    everyone = lax.all_gather(both_tokens, "row", axis=0, tiled=True)
    logits = jnp.einsum("ijk,kh->hji", pair, pair_weight, preferred_element_type=jnp.float32)
    local_max = jnp.max(logits, axis=1)
    local_total = jnp.sum(jnp.exp(logits - local_max[:, None, :]), axis=1)
    joined = exchange(jnp.stack([local_max, local_total]), ("col",), join_softmax, 1)
    probs = jnp.exp(logits - joined[0][:, None, :]) / joined[1][:, None, :]
    probs_low = probs.astype(jnp.bfloat16)
    probs_low = jnp.concatenate([probs_low, lax.ppermute(probs_low, "col", partners)], axis=1)

    v = jnp.dot(everyone.reshape(-1, width), entries, preferred_element_type=jnp.float32)
    v = v.astype(jnp.bfloat16).reshape(blocks // 2, strands, 2 * tokens, heads, head_width)
    v = v.transpose(3, 2, 0, 1, 4).reshape(heads, 2 * tokens, blocks // 2 * lanes)
    f = everyone.transpose(1, 3, 0, 2).reshape(strands * width, blocks * tokens)

    d_own, d_other = d_probs_of(g, v)
    d_probs = d_own + lax.ppermute(d_other, "col", partners).astype(jnp.float32)
    crossed = value_weight_of(g, probs_low, f, strands)
    row_dot = exchange(jnp.sum(probs * d_probs, axis=1), ("col",), add_up, 2)
    d_logits = (probs * (d_probs - row_dot[:, None, :])).astype(jnp.bfloat16)
    d_pair, d_pair_weight = pair_gradients(
        d_logits.transpose(0, 2, 1).reshape(heads, rows * tokens),
        pair.reshape(rows * tokens, pair_width), pair_weight.T)
    d_value_weight = crossed.reshape(width, heads, strands, head_width).sum(2)
    both = jnp.concatenate([d_pair_weight.reshape(-1), d_value_weight.reshape(-1)]).reshape(-1, 128)
    both = exchange(both, ("row",), add_up, 3)
    both = exchange(both, ("col",), add_up, 4).reshape(-1)
    both = both * (1.0 / token_total)
    cut = heads * pair_width
    return (
        d_pair.reshape(pair.shape),
        both[:cut].reshape(heads, pair_width).T,
        both[cut:].reshape(width, width),
    )


def solution(mesh):
    placed = (P("row", "col", None), P(), P("row", "col", None), P("col", "row", None), P())
    return jax.shard_map(
        on_device,
        mesh=mesh,
        in_specs=placed,
        out_specs=(P("row", "col", None), P(), P()),
        check_vma=False,
    )
```

profile of v0, /device:TPU:12, one launch (start us, length us, event | category | flops | bytes accessed | tf_op | source)
XLA Modules:
  0.0 272.8 jit_solution(14530640087173472015)
XLA Ops:
  7.2 0.0 copy-start
  7.2 0.0 all-gather.5.cloned.1.call-start
  7.2 4.0 %copy.36 = bf16[128,64,64]{2,1,0:T(8,128)(2,1)S(1)} copy(bf16[128,64,64]{0,2,1:T(8,128)(2,1)} %param.7) | data formatting | bytes 2097152 | tf_op args[2]
  11.3 0.2 dynamic-slice_bitcast_fusion.1
  11.5 1.6 collective-permute-start
  13.0 23.4 %collective-permute-done = bf16[4,16,64,64]{3,2,1,0:T(8,128)(2,1)S(1)} collective-permute-done((bf16[4,16,64,64]{3,2,1,0:T(8,128)(2,1)S(1)}, bf16[4,16,64,64]{3,2,1,0:T(8,128)(2,1)S(1)}, u32[]{:S(2)}, u32[]{:S(2)}) %collective-permute-start) | collective-permute-done | bytes 524320 | tf_op jit(solution)/shard_map/ppermute | solution.py:221
  36.4 0.6 pad_maximum_fusion
  37.0 1.6 copy.37
  38.6 0.0 all-gather.5.cloned.1.call-update
  38.6 0.0 all-gather.3.cloned.1.call-start
  38.7 0.0 copy-done
  38.7 0.1 copy_bitcast_fusion.1
  38.8 0.0 copy-start.2
  38.8 1.3 copy.35
  40.1 0.0 all-gather.3.cloned.1.call-update
  40.1 0.0 copy-done.2
  40.1 21.4 %fusion = f32[8,512,64]{1,0,2:T(8,128)} fusion(bf16[512,64,128]{2,1,0:T(8,128)(2,1)} %param.5, bf16[128,8]{0,1:T(8,128)(2,1)S(1)} %copy-done.2), kind=kOutput, calls=%fused_computation.1 | convolution fusion | flops 67108864 | bytes 9439232 | tf_op jit(solution)/shard_map/ijk,kh->hji/dot_general | solution.py:228
  61.6 0.0 copy-start.5
  61.6 0.0 all-gather.5.cloned.1.call-done
  61.6 3.2 %copy.38 = bf16[8,16,128,64]{2,1,0,3:T(8,128)(2,1)S(1)} copy(bf16[8,16,128,64]{2,3,1,0:T(8,128)(2,1)} %all-gather.5.cloned.1.call-done) | data formatting | bytes 4194304 | tf_op jit(solution)/shard_map/all_gather | solution.py:227
  64.8 0.0 copy-done.5
  64.8 3.0 %fusion.4 = bf16[8,128,1024]{1,2,0:T(8,128)(2,1)} fusion(bf16[64,64]{1,0:T(8,128)(2,1)S(1)} %copy-done.5, bf16[8,8,128,128]{3,2,1,0:T(8,128)(2,1)S(1)} %bitcast.76), kind=kOutput, calls=%fused_computation.7 | convolution fusion | flops 135266304 | bytes 4202496 | tf_op jit(solution)/shard_map/dot_general | solution.py:236
  67.8 2.9 %copy.39.v = bf16[8,128,1024]{2,1,0:T(8,128)(2,1)S(1)} copy(bf16[8,128,1024]{1,2,0:T(8,128)(2,1)} %fusion.4) | data formatting | bytes 4194304 | tf_op jit(solution)/shard_map/reshape | solution.py:238
  70.7 105.2 %all-gather.3.cloned.1.call-done.g = bf16[8,8,512,128]{3,2,1,0:T(8,128)(2,1)} async-done(((bf16[1,8,512,128]{3,2,1,0:T(8,128)(2,1)}), bf16[8,8,512,128]{3,2,1,0:T(8,128)(2,1)}) %all-gather.3.cloned.1.call-update) | async-done | bytes 8388624 | tf_op jit(solution)/shard_map/all_gather | solution.py:225
  175.9 0.0 copy-start.3
  175.9 7.8 %shard_map.77 = (f32[8,64,512]{2,1,0:T(8,128)S(1)}, bf16[8,64,512]{2,1,0:T(8,128)(2,1)S(1)}) custom-call(bf16[8,8,512,128]{3,2,1,0:T(8,128)(2,1)} %all-gather.3.cloned.1.call-done.g, bf16[8,128,1024]{2,1,0:T(8,128)(2,1)S(1)} %copy.39.v), custom_call_target="tpu_custom_call" | custom-call | flops 1073741824 | bytes 8388608 | tf_op jit(solution)/shard_map/pallas_call | solution.py:112
  183.7 1.6 collective-permute-start.1
  185.3 0.0 copy-done.3
  185.3 0.6 bitcast_reduce_fusion
  185.9 0.7 fusion.8
  186.6 17.5 %shard_map.76 = f32[2,8,512]{2,1,0:T(8,128)S(1)} custom-call(f32[2,8,512]{2,1,0:T(8,128)S(1)} %pad_maximum_fusion.2.mine), custom_call_target="tpu_custom_call" | custom-call | tf_op jit(solution)/shard_map/pallas_call | solution.py:72
  204.1 0.0 collective-permute-done.1
  204.1 0.8 multiply_reduce_fusion.mine
  204.9 0.0 copy-start.4
  204.9 11.5 %shard_map.78 = f32[8,512]{1,0:T(8,128)S(1)} custom-call(f32[8,512]{1,0:T(8,128)S(1)} %multiply_reduce_fusion.mine), custom_call_target="tpu_custom_call" | custom-call | tf_op jit(solution)/shard_map/pallas_call | solution.py:72
  216.4 1.8 fusion.13
  218.2 1.5 collective-permute-start.2
  219.7 0.0 copy-done.4
  219.7 1.8 copy.41
  221.5 0.6 copy.65
  222.1 2.4 copy.40
  224.5 2.9 %reshape.63.d_logits = bf16[8,32768]{1,0:T(8,128)(2,1)} reshape(bf16[8,512,64]{2,1,0:T(8,128)(2,1)} %copy.40) | data formatting | bytes 1048576 | tf_op jit(solution)/shard_map/reshape | solution.py:247
  227.4 0.0 copy-start.1
  227.4 1.0 copy-done.1
  228.4 10.5 %shard_map.79 = (bf16[32768,128]{1,0:T(8,128)(2,1)}, f32[8,128]{1,0:T(8,128)S(1)}) custom-call(bf16[8,32768]{1,0:T(8,128)(2,1)S(1)} %copy-done.1, bf16[32768,128]{1,0:T(8,128)(2,1)} %bitcast.75, bf16[8,128]{1,0:T(8,128)(2,1)S(1)} %bitcast.73), custom_call_target="tpu_custom_call" | custom-call | tf_op jit(solution)/shard_map/pallas_call | solution.py:189
  238.9 0.0 collective-permute-done.2
  238.9 1.3 pad_maximum_fusion.1.p
  240.2 9.7 %shard_map.80 = f32[64,1024]{1,0:T(8,128)S(1)} custom-call(bf16[8,8,512,128]{3,2,1,0:T(8,128)(2,1)} %all-gather.3.cloned.1.call-done.g, bf16[8,128,512]{2,1,0:T(8,128)(2,1)S(1)} %pad_maximum_fusion.1.p, bf16[1024,1024]{1,0:T(8,128)(2,1)S(1)} %bitcast.72), custom_call_target="tpu_custom_call" | custom-call | flops 2147483648 | bytes 8388608 | tf_op jit(solution)/shard_map/pallas_call | solution.py:157
  249.9 0.2 copy.42
  250.1 0.1 copy.43
  250.3 0.1 reshape.69
  250.5 1.3 shard_map.81.mine
  251.7 12.9 %shard_map.82 = f32[40,128]{1,0:T(8,128)S(1)} custom-call(f32[40,128]{1,0:T(8,128)S(1)} %shard_map.81.mine), custom_call_target="tpu_custom_call" | custom-call | tf_op jit(solution)/shard_map/pallas_call | solution.py:72
  264.7 0.6 slice_bitcast_fusion.2
  265.3 0.7 slice.21
  (6 shorter events, 0.1 us)
Async XLA Ops:
  7.2 31.5 %copy-start = (bf16[16,512,64]{1,2,0:T(8,128)(2,1)S(1)}, bf16[16,512,64]{1,2,0:T(8,128)(2,1)}, u32[]{:S(2)}) copy-start(bf16[16,512,64]{1,2,0:T(8,128)(2,1)} %param.8) | copy-start | bytes 3145732
  7.2 54.4 %all-gather.5.cloned.1.call-start = ((), (), s32[]{:S(2)}) async-start(), calls=%async_computation.1 | async-start | bytes 3145728 | tf_op jit(solution)/shard_map/all_gather | solution.py:227
  11.5 25.0 %collective-permute-start = (bf16[4,16,64,64]{3,2,1,0:T(8,128)(2,1)S(1)}, bf16[4,16,64,64]{3,2,1,0:T(8,128)(2,1)S(1)}, u32[]{:S(2)}, u32[]{:S(2)}) collective-permute-start(bf16[4,16,64,64]{3,2,1,0:T(8,128)(2,1)S(1)} %get-tuple-element.12), channel_id=1, source_target_pairs={{0,1},{1,0},{2,3},{3,2},{4,5},{5,4},{6,7},{7,6},{8,9},{9,8},{10,11... | collective-permute-start | bytes 1572872 | tf_op jit(solution)/shard_map/ppermute | solution.py:221
  38.6 137.3 %all-gather.3.cloned.1.call-start = ((), (), s32[]{:S(2)}) async-start(), calls=%async_computation | async-start | bytes 9437184 | tf_op jit(solution)/shard_map/all_gather | solution.py:225
  38.8 1.3 copy-start.2
  61.6 3.2 %copy-start.5 = (bf16[64,64]{1,0:T(8,128)(2,1)S(1)}, bf16[64,64]{1,0:T(8,128)(2,1)}, u32[]{:S(2)}) copy-start(bf16[64,64]{1,0:T(8,128)(2,1)} %param.9) | copy-start | bytes 24580
  175.9 9.4 %copy-start.3 = (f32[8,512,64]{1,0,2:T(8,128)S(1)}, f32[8,512,64]{1,0,2:T(8,128)}, u32[]{:S(2)}) copy-start(f32[8,512,64]{1,0,2:T(8,128)} %fusion) | copy-start | bytes 3145732
  183.7 20.4 %collective-permute-start.1 = (bf16[8,64,512]{2,1,0:T(8,128)(2,1)S(1)}, bf16[8,64,512]{2,1,0:T(8,128)(2,1)S(1)}, u32[]{:S(2)}, u32[]{:S(2)}) collective-permute-start(bf16[8,64,512]{2,1,0:T(8,128)(2,1)S(1)} %get-tuple-element.8), channel_id=1, source_target_pairs={{0,1},{1,0},{2,3},{3,2},{4,5},{5,4},{6,7},{7,6},{8,9},{9,8},{10,11... | collective-permute-start | bytes 1572872 | tf_op jit(solution)/shard_map/ppermute | solution.py:242
  204.9 14.8 %copy-start.4 = (bf16[8,16,128,64]{2,3,1,0:T(8,128)(2,1)S(1)}, bf16[8,16,128,64]{2,3,1,0:T(8,128)(2,1)}, u32[]{:S(2)}) copy-start(bf16[8,16,128,64]{2,3,1,0:T(8,128)(2,1)} %all-gather.5.cloned.1.call-done) | copy-start | bytes 6291460
  218.2 20.7 %collective-permute-start.2 = (bf16[8,64,512]{2,1,0:T(8,128)(2,1)}, bf16[8,64,512]{2,1,0:T(8,128)(2,1)}, u32[]{:S(2)}, u32[]{:S(2)}) collective-permute-start(bf16[8,64,512]{2,1,0:T(8,128)(2,1)} %get-tuple-element.13), channel_id=1, source_target_pairs={{0,1},{1,0},{2,3},{3,2},{4,5},{5,4},{6,7},{7,6},{8,9},{9,8},{10,11... | collective-permute-start | bytes 1572872 | tf_op jit(solution)/shard_map/ppermute | solution.py:234
  227.4 1.0 copy-start.1
Sparse Core Ops, SparseCore 0:
  38.8 11.9 all-gather.4
  52.9 122.9 all-gather.2
where the time goes:
time: 274 us; the launch traced here: 273 us
  waiting for transfers between devices  129 us (47%)
  Pallas kernels  71.2 us (26%)
  matrix products  24.4 us (9%)
  local copies, waits for them, and re-layouts  23.7 us (9%)
  between operations  14.3 us (5%)
  other arithmetic  5.75 us (2%)
  starting transfers between devices  4.73 us (2%)
    all_gather x1, waiting for transfers between devices, on_device(): g = lax.all_gather(g, 'col', axis=0, axis_index_groups=groups)  105 us
    pallas_call x4, Pallas kernels, exchange(): pl.pallas_call(functools.partial(exchange_kernel, axes, combine), out_sha...  43.2 us
    ppermute x1, waiting for transfers between devices, on_device(): lax.ppermute(sent, 'col', partners)  23.4 us
    dot_general x1, matrix products, on_device(): jnp.einsum('ijk,kh->hji', pair, pair_weight, preferred_element_type=jnp.f...  21.4 us
    pallas_call x1, Pallas kernels, pair_gradients(): pl.pallas_call(pair_kernel, grid=(cells // block,), in_specs=[pl.BlockSpe...  10.5 us
    pallas_call x1, Pallas kernels, value_weight_of(): pl.pallas_call(functools.partial(value_kernel, heads, strands), grid=(ste...  9.68 us
    pallas_call x1, Pallas kernels, d_probs_of(): pl.pallas_call(functools.partial(d_probs_kernel, heads, tokens // 2), gri...  7.77 us
    unnamed x14, local copies, waits for them, and re-layouts  5.7 us
  transfers between devices with their start and end apart: 5, of which 2 were waited for; matrix products, arithmetic and copies ran while one was open for 15% of the time, Pallas kernels for 10%

commit v1 on v0

--- a/solution.py
+++ b/solution.py
@@ -215,16 +215,23 @@
     groups = [list(range(q, blocks, 2)) for q in range(2)]
     partners = [(c, c ^ 1) for c in range(blocks)]
 
+    g = sensitivity.reshape(strands, rows, heads, head_width)
+    g = g.transpose(2, 1, 0, 3).reshape(heads, rows, lanes)
+    g, features, pair = lax.optimization_barrier((g, features, pair))
+    g = lax.all_gather(g, "col", axis=0, axis_index_groups=groups)
+
     features = features.reshape(-1, 2, strands, tokens, width)
     kept = lax.dynamic_index_in_dim(features, parity, 1, keepdims=False)
     sent = lax.dynamic_index_in_dim(features, 1 - parity, 1, keepdims=False)
     both_tokens = jnp.concatenate([kept, lax.ppermute(sent, "col", partners)], axis=2)
-
-    g = sensitivity.reshape(strands, rows, heads, head_width)
-    g = g.transpose(2, 1, 0, 3).reshape(heads, rows, lanes)
-    g = lax.all_gather(g, "col", axis=0, axis_index_groups=groups)
-
-    everyone = lax.all_gather(both_tokens, "row", axis=0, tiled=True)
+    row, row_count = lax.axis_index("row"), lax.axis_size("row")
+    everyone = jnp.zeros((row_count,) + both_tokens.shape, both_tokens.dtype)
+    for d in range(row_count):
+        part = both_tokens
+        if d:
+            part = lax.ppermute(part, "row", [(r, (r + d) % row_count) for r in range(row_count)])
+        everyone = lax.dynamic_update_index_in_dim(everyone, part, (row - d) % row_count, 0)
+    everyone = everyone.reshape((-1,) + both_tokens.shape[1:])
     logits = jnp.einsum("ijk,kh->hji", pair, pair_weight, preferred_element_type=jnp.float32)
     local_max = jnp.max(logits, axis=1)
     local_total = jnp.sum(jnp.exp(logits - local_max[:, None, :]), axis=1)
@@ -238,6 +245,7 @@
     v = v.transpose(3, 2, 0, 1, 4).reshape(heads, 2 * tokens, blocks // 2 * lanes)
     f = everyone.transpose(1, 3, 0, 2).reshape(strands * width, blocks * tokens)
 
+    g, v, f, probs, probs_low = lax.optimization_barrier((g, v, f, probs, probs_low))
     d_own, d_other = d_probs_of(g, v)
     d_probs = d_own + lax.ppermute(d_other, "col", partners).astype(jnp.float32)
     crossed = value_weight_of(g, probs_low, f, strands)

time: 274 us -> 222 us (0.81)
  waiting for transfers between devices: 129 us -> 59.1 us
  Pallas kernels: 71.2 us -> 84.1 us
  matrix products: 24.4 us -> 13.6 us
  other arithmetic: 5.75 us -> 14.2 us
  local copies, waits for them, and re-layouts: 23.7 us -> 29.7 us
    all_gather x1, waiting for transfers between devices: 105 us -> 50.2 us  [on_device(): g = lax.all_gather(g, 'col', axis=0, axis_index_groups=groups)]
    ppermute x1, waiting for transfers between devices: 23.4 us -> 0.01 us  [on_device(): lax.ppermute(sent, 'col', partners)]
    pallas_call x4, Pallas kernels: 43.2 us -> 54.9 us  [exchange(): pl.pallas_call(functools.partial(exchange_kernel, axes, combine), out_sha...]
    dot_general x1, matrix products: 21.4 us -> 10.6 us  [on_device(): jnp.einsum('ijk,kh->hji', pair, pair_weight, preferred_element_type=jnp.f...]
    ppermute x1, waiting for transfers between devices: 0.01 us -> 8.91 us  [on_device(): lax.ppermute(probs_low, 'col', partners)]
    optimization_barrier x0 -> x3, local copies, waits for them, and re-layouts: none -> 8.16 us  [the longest x2 5.3 us: on_device(): g, features, pair = lax.optimization_barrier((g, features, pair))]
    concatenate x1, other arithmetic: 0.57 us -> 4.47 us  [on_device(): jnp.concatenate([kept, lax.ppermute(sent, 'col', partners)], axis=2)]
    broadcast_in_dim x0 -> x2, local copies, waits for them, and re-layouts: none -> 3.38 us  [the longest x1 2.87 us: on_device(): lax.dynamic_update_index_in_dim(everyone, part, (row - d) % row_count, 0)]
  transfers between devices with their start and end apart: 5 -> 5, of which waited for: 2 -> 2; matrix products, arithmetic and copies ran while one was open for 15% -> 20% of each run, Pallas kernels for 10% -> 18%
where the time goes in v1:
time: 222 us; the launch traced here: 221 us
  Pallas kernels  84.1 us (38%)
  waiting for transfers between devices  59.1 us (27%)
  local copies, waits for them, and re-layouts  29.7 us (13%)
  between operations  14.3 us (6%)
  other arithmetic  14.2 us (6%)
  matrix products  13.6 us (6%)
  starting transfers between devices  6.17 us (3%)
    pallas_call x4, Pallas kernels, exchange(): pl.pallas_call(functools.partial(exchange_kernel, axes, combine), out_sha...  54.9 us
    all_gather x1, waiting for transfers between devices, on_device(): g = lax.all_gather(g, 'col', axis=0, axis_index_groups=groups)  50.2 us
    dot_general x1, matrix products, on_device(): jnp.einsum('ijk,kh->hji', pair, pair_weight, preferred_element_type=jnp.f...  10.6 us
    pallas_call x1, Pallas kernels, pair_gradients(): pl.pallas_call(pair_kernel, grid=(cells // block,), in_specs=[pl.BlockSpe...  10.5 us
    pallas_call x1, Pallas kernels, value_weight_of(): pl.pallas_call(functools.partial(value_kernel, heads, strands), grid=(ste...  9.89 us
    ppermute x1, waiting for transfers between devices, on_device(): lax.ppermute(probs_low, 'col', partners)  8.91 us
    pallas_call x1, Pallas kernels, d_probs_of(): pl.pallas_call(functools.partial(d_probs_kernel, heads, tokens // 2), gri...  8.85 us
    optimization_barrier x2, local copies, waits for them, and re-layouts, on_device(): g, features, pair = lax.optimization_barrier((g, features, pair))  5.3 us
  transfers between devices with their start and end apart: 5, of which 2 were waited for; matrix products, arithmetic and copies ran while one was open for 20% of the time, Pallas kernels for 18%

profile of v1, /device:TPU:12, one launch (start us, length us, event | category | flops | bytes accessed | tf_op | source)
XLA Modules:
  0.0 221.2 jit_solution(15852425786094722568)
XLA Ops:
  7.2 0.0 copy-start
  7.2 0.0 all-gather.3.cloned.1.call-start
  7.2 1.2 copy-done
  8.4 0.1 copy_bitcast_fusion.1
  8.5 1.4 copy.34
  9.8 0.0 all-gather.3.cloned.1.call-update
  9.9 3.9 %copy.35 = bf16[128,64,64]{2,1,0:T(8,128)(2,1)S(1)} copy(bf16[128,64,64]{0,2,1:T(8,128)(2,1)} %param.7) | data formatting | bytes 2097152 | tf_op jit(solution)/shard_map/optimization_barrier | solution.py:220
  13.8 0.0 copy-start.5
  13.9 1.6 dynamic-slice_bitcast_fusion.1
  15.5 1.5 collective-permute-start
  17.0 0.0 copy-done.5
  17.0 10.6 %fusion.10 = f32[512,64,8]{1,2,0:T(8,128)S(1)} fusion(bf16[512,64,128]{2,1,0:T(8,128)(2,1)} %param.5, bf16[128,8]{0,1:T(8,128)(2,1)S(1)} %copy-done.5), kind=kOutput, calls=%fused_computation.28 | convolution fusion | flops 67108864 | bytes 9439232 | tf_op jit(solution)/shard_map/ijk,kh->hji/dot_general | solution.py:235
  27.6 1.7 copy.40
  29.3 1.4 bitcast_reduce_fusion
  30.7 1.4 fusion.6
  32.1 29.3 %shard_map.76 = f32[2,8,512]{2,1,0:T(8,128)S(1)} custom-call(f32[2,8,512]{2,1,0:T(8,128)S(1)} %pad_maximum_fusion.2.mine), custom_call_target="tpu_custom_call" | custom-call | tf_op jit(solution)/shard_map/pallas_call | solution.py:72
  61.5 0.0 collective-permute-done
  61.5 0.0 copy-done.8
  61.5 4.5 %pad_maximum_fusion = (bf16[4,16,128,64]{3,2,1,0:T(8,128)(2,1)}, bf16[1,4,16,128,64]{4,3,2,1,0:T(8,128)(2,1)}) fusion(bf16[4,16,64,64]{3,2,1,0:T(8,128)(2,1)} %collective-permute-done, bf16[4,16,64,64]{3,2,1,0:T(8,128)(2,1)S(1)} %copy-done.8), kind=kLoop, calls=%fused_computation.4 | loop fusion | flops 2097152 | bytes 3145728 | tf_op jit(solution)/shard_map/concatenate | solution.py:226
  66.0 2.8 %copy.37 = bf16[4,16,128,64]{2,3,1,0:T(8,128)(2,1)} copy(bf16[4,16,128,64]{3,2,1,0:T(8,128)(2,1)} %get-tuple-element.29) | data formatting | bytes 2097152 | tf_op jit(solution)/shard_map/concatenate | solution.py:226
  68.7 0.0 collective-permute-start.1
  68.7 0.0 copy-done.6
  68.8 1.2 fusion.13
  69.9 3.1 %collective-permute-start.2 = (bf16[8,64,512]{2,1,0:T(8,128)(2,1)S(1)}, bf16[8,64,512]{2,1,0:T(8,128)(2,1)S(1)}, u32[]{:S(2)}, u32[]{:S(2)}) collective-permute-start(bf16[8,64,512]{2,1,0:T(8,128)(2,1)S(1)} %get-tuple-element.27), channel_id=1, source_target_pairs={{0,1},{1,0},{2,3},{3,2},{4,5},{5,4},{6,7},{7,6},{8,9},{9,8},{10,11... | collective-permute-start | bytes 1572872 | tf_op jit(solution)/shard_map/ppermute | solution.py:241
  73.0 2.9 %copy.36 = bf16[1,4,16,128,64]{3,2,1,0,4:T(8,128)(2,1)S(1)} copy(bf16[1,4,16,128,64]{4,3,2,1,0:T(8,128)(2,1)} %get-tuple-element.30) | data formatting | bytes 2097152 | tf_op jit(solution)/shard_map/jit(dynamic_update_index_in_dim)/broadcast_in_dim | solution.py:233
  75.9 0.5 broadcast_in_dim.12
  76.4 0.3 constant_dynamic-update-slice_fusion
  76.7 8.9 %collective-permute-done.2 = bf16[8,64,512]{2,1,0:T(8,128)(2,1)S(1)} collective-permute-done((bf16[8,64,512]{2,1,0:T(8,128)(2,1)S(1)}, bf16[8,64,512]{2,1,0:T(8,128)(2,1)S(1)}, u32[]{:S(2)}, u32[]{:S(2)}) %collective-permute-start.2) | collective-permute-done | bytes 524320 | tf_op jit(solution)/shard_map/ppermute | solution.py:241
  85.6 1.1 pad_maximum_fusion.1.p
  86.7 0.0 collective-permute-done.1
  86.7 2.0 copy_dynamic-update-slice_fusion
  88.7 0.5 copy.39
  89.2 0.0 copy-start.9
  89.2 2.1 copy.56
  91.3 0.0 copy-done.9
  91.3 3.0 %fusion.2 = bf16[8,128,1024]{1,2,0:T(8,128)(2,1)} fusion(bf16[64,64]{1,0:T(8,128)(2,1)S(1)} %copy-done.9, bf16[8,8,128,128]{3,2,1,0:T(8,128)(2,1)S(1)} %bitcast.80), kind=kOutput, calls=%fused_computation.5 | convolution fusion | flops 135266304 | bytes 4202496 | tf_op jit(solution)/shard_map/dot_general | solution.py:243
  94.3 50.2 %all-gather.3.cloned.1.call-done = bf16[64,512,128]{2,1,0:T(8,128)(2,1)} async-done(((bf16[8,512,128]{2,1,0:T(8,128)(2,1)}), bf16[64,512,128]{2,1,0:T(8,128)(2,1)}) %all-gather.3.cloned.1.call-update) | async-done | bytes 8388624 | tf_op jit(solution)/shard_map/all_gather | solution.py:221
  144.5 2.9 %copy.41.v = bf16[8,128,1024]{2,1,0:T(8,128)(2,1)S(1)} copy(bf16[8,128,1024]{1,2,0:T(8,128)(2,1)} %fusion.2) | data formatting | bytes 4194304 | tf_op jit(solution)/shard_map/optimization_barrier | solution.py:248
  147.3 0.0 copy-start.1
  147.3 0.0 copy-start.2
  147.3 8.8 %shard_map.77 = (f32[8,64,512]{2,1,0:T(8,128)S(1)}, bf16[8,64,512]{2,1,0:T(8,128)(2,1)}) custom-call(bf16[8,8,512,128]{3,2,1,0:T(8,128)(2,1)} %bitcast.77, bf16[8,128,1024]{2,1,0:T(8,128)(2,1)S(1)} %copy.41.v), custom_call_target="tpu_custom_call" | custom-call | flops 1073741824 | bytes 8388608 | tf_op jit(solution)/shard_map/pallas_call | solution.py:112
  156.2 1.0 copy-done.3
  157.2 1.6 collective-permute-start.3
  158.7 0.0 copy-done.1
  158.7 0.0 copy-done.2
  158.7 9.9 %shard_map.80 = f32[64,1024]{1,0:T(8,128)S(1)} custom-call(bf16[8,8,512,128]{3,2,1,0:T(8,128)(2,1)} %bitcast.78, bf16[8,128,512]{2,1,0:T(8,128)(2,1)S(1)} %copy-done.2, bf16[1024,1024]{1,0:T(8,128)(2,1)S(1)} %bitcast.73), custom_call_target="tpu_custom_call" | custom-call | flops 2147483648 | bytes 8388608 | tf_op jit(solution)/shard_map/pallas_call | solution.py:157
  168.6 0.0 copy-start.4
  168.6 1.0 copy.43
  169.6 1.1 reduce_sum.29
  170.7 0.1 copy.44
  170.9 0.1 reshape.73
  171.0 0.0 collective-permute-done.3
  171.0 0.0 copy-done.7
  171.0 0.0 copy-done.4
  171.0 1.4 multiply_reduce_fusion.mine
  172.4 11.5 %shard_map.78 = f32[8,512]{1,0:T(8,128)S(1)} custom-call(f32[8,512]{1,0:T(8,128)S(1)} %multiply_reduce_fusion.mine), custom_call_target="tpu_custom_call" | custom-call | tf_op jit(solution)/shard_map/pallas_call | solution.py:72
  183.9 2.2 fusion.9
  186.1 1.5 copy.42
  187.6 0.8 reshape.68.d_logits
  188.5 10.5 %shard_map.79 = (bf16[32768,128]{1,0:T(8,128)(2,1)}, f32[8,128]{1,0:T(8,128)S(1)}) custom-call(bf16[8,32768]{1,0:T(8,128)(2,1)S(1)} %reshape.68.d_logits, bf16[32768,128]{1,0:T(8,128)(2,1)} %bitcast.76, bf16[8,128]{1,0:T(8,128)(2,1)S(1)} %bitcast.74), custom_call_target="tpu_custom_call" | custom-call | tf_op jit(solution)/shard_map/pallas_call | solution.py:189
  198.9 1.2 shard_map.81.mine
  200.2 12.9 %shard_map.82 = f32[40,128]{1,0:T(8,128)S(1)} custom-call(f32[40,128]{1,0:T(8,128)S(1)} %shard_map.81.mine), custom_call_target="tpu_custom_call" | custom-call | tf_op jit(solution)/shard_map/pallas_call | solution.py:72
  213.1 0.6 slice_bitcast_fusion.2
  213.7 0.7 slice.21
  (9 shorter events, 0.0 us)
Async XLA Ops:
  7.2 1.2 copy-start
  7.2 137.3 %all-gather.3.cloned.1.call-start = ((), (), s32[]{:S(2)}) async-start(), calls=%async_computation | async-start | bytes 9437184 | tf_op jit(solution)/shard_map/all_gather | solution.py:221
  13.8 3.1 %copy-start.5 = (bf16[128,8]{0,1:T(8,128)(2,1)S(1)}, bf16[128,8]{0,1:T(8,128)(2,1)}, u32[]{:S(2)}) copy-start(bf16[128,8]{0,1:T(8,128)(2,1)} %param.6) | copy-start | bytes 6148
  15.5 46.0 %collective-permute-start = (bf16[4,16,64,64]{3,2,1,0:T(8,128)(2,1)}, bf16[4,16,64,64]{3,2,1,0:T(8,128)(2,1)}, u32[]{:S(2)}, u32[]{:S(2)}) collective-permute-start(bf16[4,16,64,64]{3,2,1,0:T(8,128)(2,1)} %get-tuple-element.32), channel_id=1, source_target_pairs={{0,1},{1,0},{2,3},{3,2},{4,5},{5,4},{6,7},{7,6},{8,9},{9,8},{10,11... | collective-permute-start | bytes 1572872 | tf_op jit(solution)/shard_map/ppermute | solution.py:226
  29.3 32.2 %copy-start.8 = (bf16[4,16,64,64]{3,2,1,0:T(8,128)(2,1)S(1)}, bf16[4,16,64,64]{3,2,1,0:T(8,128)(2,1)}, u32[]{:S(2)}) copy-start(bf16[4,16,64,64]{3,2,1,0:T(8,128)(2,1)} %get-tuple-element.31) | copy-start | bytes 1572868
  65.9 2.8 %copy-start.6 = (f32[512,64,8]{0,1,2:T(8,128)S(1)}, f32[512,64,8]{0,1,2:T(8,128)}, u32[]{:S(2)}) copy-start(f32[512,64,8]{0,1,2:T(8,128)} %copy.40) | copy-start | bytes 3145732
  68.7 18.0 %collective-permute-start.1 = (bf16[4,16,128,64]{2,3,1,0:T(8,128)(2,1)}, bf16[4,16,128,64]{2,3,1,0:T(8,128)(2,1)}, u32[]{:S(2)}, u32[]{:S(2)}) collective-permute-start(bf16[4,16,128,64]{2,3,1,0:T(8,128)(2,1)} %copy.37), channel_id=1, source_target_pairs={{0,16},{16,0},{1,17},{17,1},{2,18},{18,2},{3,19},{19,3},{4,20},{20... | collective-permute-start | bytes 3145736 | tf_op jit(solution)/shard_map/ppermute | solution.py:232
  69.9 15.7 %collective-permute-start.2 = (bf16[8,64,512]{2,1,0:T(8,128)(2,1)S(1)}, bf16[8,64,512]{2,1,0:T(8,128)(2,1)S(1)}, u32[]{:S(2)}, u32[]{:S(2)}) collective-permute-start(bf16[8,64,512]{2,1,0:T(8,128)(2,1)S(1)} %get-tuple-element.27), channel_id=1, source_target_pairs={{0,1},{1,0},{2,3},{3,2},{4,5},{5,4},{6,7},{7,6},{8,9},{9,8},{10,11... | collective-permute-start | bytes 1572872 | tf_op jit(solution)/shard_map/ppermute | solution.py:241
  89.2 2.1 copy-start.9
  147.3 11.4 %copy-start.1 = (bf16[128,8,8,128]{3,1,2,0:T(8,128)(2,1)S(1)}, bf16[128,8,8,128]{3,1,2,0:T(8,128)(2,1)}, u32[]{:S(2)}) copy-start(bf16[128,8,8,128]{3,1,2,0:T(8,128)(2,1)} %copy.56) | copy-start | bytes 6291460
  147.3 11.4 %copy-start.2 = (bf16[8,128,512]{2,1,0:T(8,128)(2,1)S(1)}, bf16[8,128,512]{2,1,0:T(8,128)(2,1)}, u32[]{:S(2)}) copy-start(bf16[8,128,512]{2,1,0:T(8,128)(2,1)} %pad_maximum_fusion.1.p) | copy-start | bytes 3145732
  156.2 1.0 copy-start.3
  157.2 13.9 %collective-permute-start.3 = (bf16[8,64,512]{2,1,0:T(8,128)(2,1)}, bf16[8,64,512]{2,1,0:T(8,128)(2,1)}, u32[]{:S(2)}, u32[]{:S(2)}) collective-permute-start(bf16[8,64,512]{2,1,0:T(8,128)(2,1)} %get-tuple-element.22), channel_id=1, source_target_pairs={{0,1},{1,0},{2,3},{3,2},{4,5},{5,4},{6,7},{7,6},{8,9},{9,8},{10,11... | collective-permute-start | bytes 1572872 | tf_op jit(solution)/shard_map/ppermute | solution.py:250
  158.7 12.3 %copy-start.7 = (f32[8,64,512]{2,1,0:T(8,128)S(1)}, f32[8,64,512]{2,1,0:T(8,128)}, u32[]{:S(2)}) copy-start(f32[8,64,512]{2,1,0:T(8,128)} %get-tuple-element.18) | copy-start | bytes 3145732
  168.6 2.4 %copy-start.4 = (f32[8,64,512]{2,1,0:T(8,128)S(1)}, f32[8,64,512]{2,1,0:T(8,128)}, u32[]{:S(2)}) copy-start(f32[8,64,512]{2,1,0:T(8,128)} %copy-done.3) | copy-start | bytes 3145732
Sparse Core Ops, SparseCore 0:
  10.1 134.2 all-gather.2

commit v2 on v1

--- a/solution.py
+++ b/solution.py
@@ -84,7 +84,8 @@
     )(x)
 
 
-def d_probs_kernel(heads, own, g, v, d_own, d_other, total):
+def d_probs_kernel(heads, own, g, v, d_own, *rest):
+    d_others, total = rest[:-1], rest[-1]
     step = pl.program_id(0)
 
     @pl.when(step == 0)
@@ -98,26 +99,28 @@
     @pl.when(step == pl.num_programs(0) - 1)
     def _():
         d_own[...] = total[:, :own]
-        d_other[...] = total[:, own:].astype(jnp.bfloat16)
+        for d, other in enumerate(d_others, 1):
+            other[...] = total[:, d * own:(d + 1) * own].astype(jnp.bfloat16)
 
 
 def whole(shape):
     return pl.BlockSpec(shape, lambda c: (0,) * len(shape))
 
 
-def d_probs_of(g, v):
+def d_probs_of(g, v, group):
     steps, heads, rows, lanes = g.shape
     tokens = v.shape[1]
-    half = (heads, tokens // 2, rows)
-    return pl.pallas_call(
-        functools.partial(d_probs_kernel, heads, tokens // 2),
+    share = (heads, tokens // group, rows)
+    return pl.pallas_call(
+        functools.partial(d_probs_kernel, heads, tokens // group),
         grid=(steps,),
         in_specs=[
             pl.BlockSpec((1, heads, rows, lanes), lambda c: (c, 0, 0, 0)),
             pl.BlockSpec((heads, tokens, lanes), lambda c: (0, 0, c)),
         ],
-        out_specs=[whole(half), whole(half)],
-        out_shape=[jax.ShapeDtypeStruct(half, jnp.float32), jax.ShapeDtypeStruct(half, jnp.bfloat16)],
+        out_specs=[whole(share)] * group,
+        out_shape=[jax.ShapeDtypeStruct(share, jnp.float32)]
+        + [jax.ShapeDtypeStruct(share, jnp.bfloat16)] * (group - 1),
         scratch_shapes=[pltpu.VMEM((heads, tokens, rows), jnp.float32)],
         compiler_params=pltpu.CompilerParams(vmem_limit_bytes=VMEM_BYTES),
         cost_estimate=pl.CostEstimate(
@@ -211,43 +214,48 @@
     blocks = lax.axis_size("col")
     token_total = tokens * blocks
     lanes = strands * head_width
-    parity = lax.axis_index("col") % 2
-    groups = [list(range(q, blocks, 2)) for q in range(2)]
-    partners = [(c, c ^ 1) for c in range(blocks)]
+    group = math.gcd(4, features.shape[0] // strands)
+    place = lax.axis_index("col") % group
+    groups = [list(range(q, blocks, group)) for q in range(group)]
+
+    def swap(x, d):
+        return lax.ppermute(x, "col", [(c, c ^ d) for c in range(blocks)])
+
 
     g = sensitivity.reshape(strands, rows, heads, head_width)
     g = g.transpose(2, 1, 0, 3).reshape(heads, rows, lanes)
     g, features, pair = lax.optimization_barrier((g, features, pair))
     g = lax.all_gather(g, "col", axis=0, axis_index_groups=groups)
 
-    features = features.reshape(-1, 2, strands, tokens, width)
-    kept = lax.dynamic_index_in_dim(features, parity, 1, keepdims=False)
-    sent = lax.dynamic_index_in_dim(features, 1 - parity, 1, keepdims=False)
-    both_tokens = jnp.concatenate([kept, lax.ppermute(sent, "col", partners)], axis=2)
+    features = features.reshape(-1, group, strands, tokens, width)
+    shares = [lax.dynamic_index_in_dim(features, place ^ d, 1, keepdims=False) for d in range(group)]
+    shares = shares[:1] + [swap(share, d) for d, share in enumerate(shares[1:], 1)]
+    group_tokens = jnp.concatenate(shares, axis=2)
     row, row_count = lax.axis_index("row"), lax.axis_size("row")
-    everyone = jnp.zeros((row_count,) + both_tokens.shape, both_tokens.dtype)
+    everyone = jnp.zeros((row_count,) + group_tokens.shape, group_tokens.dtype)
     for d in range(row_count):
-        part = both_tokens
+        part = group_tokens
         if d:
             part = lax.ppermute(part, "row", [(r, (r + d) % row_count) for r in range(row_count)])
         everyone = lax.dynamic_update_index_in_dim(everyone, part, (row - d) % row_count, 0)
-    everyone = everyone.reshape((-1,) + both_tokens.shape[1:])
+    everyone = everyone.reshape((-1,) + group_tokens.shape[1:])
     logits = jnp.einsum("ijk,kh->hji", pair, pair_weight, preferred_element_type=jnp.float32)
     local_max = jnp.max(logits, axis=1)
     local_total = jnp.sum(jnp.exp(logits - local_max[:, None, :]), axis=1)
     joined = exchange(jnp.stack([local_max, local_total]), ("col",), join_softmax, 1)
     probs = jnp.exp(logits - joined[0][:, None, :]) / joined[1][:, None, :]
     probs_low = probs.astype(jnp.bfloat16)
-    probs_low = jnp.concatenate([probs_low, lax.ppermute(probs_low, "col", partners)], axis=1)
+    probs_low = jnp.concatenate([probs_low] + [swap(probs_low, d) for d in range(1, group)], axis=1)
 
     v = jnp.dot(everyone.reshape(-1, width), entries, preferred_element_type=jnp.float32)
-    v = v.astype(jnp.bfloat16).reshape(blocks // 2, strands, 2 * tokens, heads, head_width)
-    v = v.transpose(3, 2, 0, 1, 4).reshape(heads, 2 * tokens, blocks // 2 * lanes)
+    v = v.astype(jnp.bfloat16).reshape(blocks // group, strands, group * tokens, heads, head_width)
+    v = v.transpose(3, 2, 0, 1, 4).reshape(heads, group * tokens, blocks // group * lanes)
     f = everyone.transpose(1, 3, 0, 2).reshape(strands * width, blocks * tokens)
 
     g, v, f, probs, probs_low = lax.optimization_barrier((g, v, f, probs, probs_low))
-    d_own, d_other = d_probs_of(g, v)
-    d_probs = d_own + lax.ppermute(d_other, "col", partners).astype(jnp.float32)
+    d_probs, *d_others = d_probs_of(g, v, group)
+    for d, other in enumerate(d_others, 1):
+        d_probs += swap(other, d).astype(jnp.float32)
     crossed = value_weight_of(g, probs_low, f, strands)
     row_dot = exchange(jnp.sum(probs * d_probs, axis=1), ("col",), add_up, 2)
     d_logits = (probs * (d_probs - row_dot[:, None, :])).astype(jnp.bfloat16)

time: 222 us -> 200 us (0.901)
  waiting for transfers between devices: 59.1 us -> 32.7 us
  starting transfers between devices: 6.17 us -> 10.9 us
  Pallas kernels: 84.1 us -> 80.7 us
  other arithmetic: 14.2 us -> 16.8 us
    all_gather x1, waiting for transfers between devices: 50.2 us -> 0.01 us  [on_device(): g = lax.all_gather(g, 'col', axis=0, axis_index_groups=groups)]
    ppermute x3 -> x9, waiting for transfers between devices: 8.91 us -> 32.7 us  [swap(): return lax.ppermute(x, 'col', [(c, c ^ d) for c in range(blocks)])]
    ppermute x3 -> x9, starting transfers between devices: 6.13 us -> 10.9 us  [swap(): return lax.ppermute(x, 'col', [(c, c ^ d) for c in range(blocks)])]
    pallas_call x1, Pallas kernels: 9.89 us -> 7.17 us  [value_weight_of(): pl.pallas_call(functools.partial(value_kernel, heads, strands), grid=(ste...]
    pallas_call x1, Pallas kernels: 8.85 us -> 6.58 us  [d_probs_of(): pl.pallas_call(functools.partial(d_probs_kernel, heads, tokens // group),...]
    unnamed x21 -> x22, local copies, waits for them, and re-layouts: 4.25 us -> 5.32 us
  transfers between devices with their start and end apart: 5 -> 11, of which waited for: 2 -> 4; matrix products, arithmetic and copies ran while one was open for 20% -> 23% of each run, Pallas kernels for 18% -> 19%
where the time goes in v2:
time: 200 us; the launch traced here: 199 us
  Pallas kernels  80.7 us (40%)
  waiting for transfers between devices  32.7 us (16%)
  local copies, waits for them, and re-layouts  30.6 us (15%)
  other arithmetic  16.8 us (8%)
  between operations  14.3 us (7%)
  matrix products  12.6 us (6%)
  starting transfers between devices  10.9 us (5%)
    pallas_call x4, Pallas kernels, exchange(): pl.pallas_call(functools.partial(exchange_kernel, axes, combine), out_sha...  56.4 us
    ppermute x9, waiting for transfers between devices, swap(): return lax.ppermute(x, 'col', [(c, c ^ d) for c in range(blocks)])  32.7 us
    ppermute x9, starting transfers between devices, swap(): return lax.ppermute(x, 'col', [(c, c ^ d) for c in range(blocks)])  10.9 us
    dot_general x1, matrix products, on_device(): jnp.einsum('ijk,kh->hji', pair, pair_weight, preferred_element_type=jnp.f...  10.6 us
    pallas_call x1, Pallas kernels, pair_gradients(): pl.pallas_call(pair_kernel, grid=(cells // block,), in_specs=[pl.BlockSpe...  10.5 us
    pallas_call x1, Pallas kernels, value_weight_of(): pl.pallas_call(functools.partial(value_kernel, heads, strands), grid=(ste...  7.17 us
    pallas_call x1, Pallas kernels, d_probs_of(): pl.pallas_call(functools.partial(d_probs_kernel, heads, tokens // group),...  6.58 us
    unnamed x22, local copies, waits for them, and re-layouts  5.32 us
  transfers between devices with their start and end apart: 11, of which 4 were waited for; matrix products, arithmetic and copies ran while one was open for 23% of the time, Pallas kernels for 19%

profile of v2, /device:TPU:12, one launch (start us, length us, event | category | flops | bytes accessed | tf_op | source)
XLA Modules:
  0.0 198.8 jit_solution(2597566366473640234)
XLA Ops:
  7.2 0.0 copy-start
  7.2 0.0 all-gather.3.cloned.1.call-start
  7.2 1.2 copy-done
  8.4 0.1 copy_bitcast_fusion
  8.5 1.4 copy.34
  9.8 0.0 all-gather.3.cloned.1.call-update
  9.9 3.9 %copy.35 = bf16[128,64,64]{2,1,0:T(8,128)(2,1)S(1)} copy(bf16[128,64,64]{0,2,1:T(8,128)(2,1)} %param.7) | data formatting | bytes 2097152 | tf_op jit(solution)/shard_map/optimization_barrier | solution.py:227
  13.9 0.0 copy-start.5
  13.9 1.4 dynamic-slice_bitcast_fusion.3
  15.3 1.5 collective-permute-start
  16.8 0.5 collective-permute-start.1
  17.3 1.5 collective-permute-start.2
  18.8 10.6 %fusion.5 = f32[512,64,8]{1,2,0:T(8,128)S(1)} fusion(bf16[512,64,128]{2,1,0:T(8,128)(2,1)} %param.5, bf16[128,8]{0,1:T(8,128)(2,1)S(1)} %copy-done.5), kind=kOutput, calls=%fused_computation.26 | convolution fusion | flops 67108864 | bytes 9439232 | tf_op jit(solution)/shard_map/ijk,kh->hji/dot_general | solution.py:242
  29.3 1.7 copy.40
  31.0 1.4 bitcast_reduce_fusion
  32.4 1.4 fusion.1
  33.9 30.5 %shard_map.76 = f32[2,8,512]{2,1,0:T(8,128)S(1)} custom-call(f32[2,8,512]{2,1,0:T(8,128)S(1)} %pad_maximum_fusion.2.mine), custom_call_target="tpu_custom_call" | custom-call | tf_op jit(solution)/shard_map/pallas_call | solution.py:72
  64.4 0.0 collective-permute-done
  64.4 0.0 collective-permute-done.1
  64.4 4.5 %pad_maximum_fusion = (bf16[2,16,256,64]{3,2,1,0:T(8,128)(2,1)}, bf16[1,2,16,256,64]{4,3,2,1,0:T(8,128)(2,1)}) fusion(bf16[2,16,64,64]{3,2,1,0:T(8,128)(2,1)} %collective-permute-done.2, bf16[2,16,64,64]{3,2,1,0:T(8,128)(2,1)} %collective-permute-done.1, bf16[2,16,64,64]{3,2,1,0:T(8,128)(2,1)} %collective-permute-done, bf16[2,16,64,64]{3,2,1,0:T(8,128)(2,1)S(1)} %copy-done.8), kind=kLoop, calls=%fused_computation.1 | loop fusion | flops 4194304 | bytes 3145728 | tf_op jit(solution)/shard_map/concatenate | solution.py:233
  68.9 2.8 %copy.37 = bf16[2,16,256,64]{2,3,1,0:T(8,128)(2,1)} copy(bf16[2,16,256,64]{3,2,1,0:T(8,128)(2,1)} %get-tuple-element.33) | data formatting | bytes 2097152 | tf_op jit(solution)/shard_map/concatenate | solution.py:233
  71.7 0.0 collective-permute-start.3
  71.7 1.2 fusion.8
  72.9 2.5 %collective-permute-start.4 = (bf16[8,64,512]{2,1,0:T(8,128)(2,1)S(1)}, bf16[8,64,512]{2,1,0:T(8,128)(2,1)S(1)}, u32[]{:S(2)}, u32[]{:S(2)}) collective-permute-start(bf16[8,64,512]{2,1,0:T(8,128)(2,1)S(1)} %get-tuple-element.31), channel_id=1, source_target_pairs={{0,1},{1,0},{2,3},{3,2},{4,5},{5,4},{6,7},{7,6},{8,9},{9,8},{10,11... | collective-permute-start | bytes 1572872 | tf_op jit(solution)/shard_map/ppermute | solution.py:222
  75.4 0.0 collective-permute-start.5
  75.4 1.5 collective-permute-start.6
  76.8 2.9 %copy.36 = bf16[1,2,16,256,64]{3,2,1,0,4:T(8,128)(2,1)S(1)} copy(bf16[1,2,16,256,64]{4,3,2,1,0:T(8,128)(2,1)} %get-tuple-element.34) | data formatting | bytes 2097152 | tf_op jit(solution)/shard_map/jit(dynamic_update_index_in_dim)/broadcast_in_dim | solution.py:240
  79.7 0.3 broadcast_in_dim.12
  80.0 0.1 constant_dynamic-update-slice_fusion
  80.1 8.1 %collective-permute-done.4 = bf16[8,64,512]{2,1,0:T(8,128)(2,1)S(1)} collective-permute-done((bf16[8,64,512]{2,1,0:T(8,128)(2,1)S(1)}, bf16[8,64,512]{2,1,0:T(8,128)(2,1)S(1)}, u32[]{:S(2)}, u32[]{:S(2)}) %collective-permute-start.4) | collective-permute-done | bytes 524320 | tf_op jit(solution)/shard_map/ppermute | solution.py:222
  88.2 12.6 %collective-permute-done.5 = bf16[8,64,512]{2,1,0:T(8,128)(2,1)} collective-permute-done((bf16[8,64,512]{2,1,0:T(8,128)(2,1)S(1)}, bf16[8,64,512]{2,1,0:T(8,128)(2,1)}, u32[]{:S(2)}, u32[]{:S(2)}) %collective-permute-start.5) | collective-permute-done | bytes 524320 | tf_op jit(solution)/shard_map/ppermute | solution.py:222
  100.8 2.8 %pad_maximum_fusion.1.p = bf16[8,256,512]{2,1,0:T(8,128)(2,1)} fusion(bf16[8,64,512]{2,1,0:T(8,128)(2,1)} %collective-permute-done.6, bf16[8,64,512]{2,1,0:T(8,128)(2,1)} %collective-permute-done.5, bf16[8,64,512]{2,1,0:T(8,128)(2,1)S(1)} %collective-permute-done.4, bf16[8,64,512]{2,1,0:T(8,128)(2,1)S(1)} %get-tuple-element.31), kind=kLoop, calls=%fused_computation.2 | loop fusion | flops 8388608 | bytes 4194304 | tf_op jit(solution)/shard_map/concatenate | solution.py:248
  103.5 0.0 collective-permute-done.3
  103.5 1.9 copy_dynamic-update-slice_fusion
  105.4 1.3 copy.45
  106.7 1.1 copy.39
  107.8 0.0 copy-start.9
  107.8 1.9 copy.46
  109.6 2.1 %convolution_convert_fusion = bf16[16384,64]{0,1:T(8,128)(2,1)} fusion(bf16[16384,64]{0,1:T(8,128)(2,1)S(1)} %bitcast.80, bf16[64,64]{1,0:T(8,128)(2,1)S(1)} %copy-done.9), kind=kOutput, calls=%fused_computation | convolution fusion | flops 135266304 | bytes 4202496 | tf_op jit(solution)/shard_map/dot_general | solution.py:250
  111.7 2.9 %copy.41.v = bf16[8,256,512]{2,1,0:T(8,128)(2,1)S(1)} copy(bf16[8,256,512]{1,2,0:T(8,128)(2,1)} %bitcast.79) | data formatting | bytes 4194304 | tf_op jit(solution)/shard_map/optimization_barrier | solution.py:255
  114.6 6.6 %shard_map.77 = (f32[8,64,512]{2,1,0:T(8,128)S(1)}, bf16[8,64,512]{2,1,0:T(8,128)(2,1)}, bf16[8,64,512]{2,1,0:T(8,128)(2,1)}, bf16[8,64,512]{2,1,0:T(8,128)(2,1)}) custom-call(bf16[4,8,512,128]{3,2,1,0:T(8,128)(2,1)} %bitcast.77, bf16[8,256,512]{2,1,0:T(8,128)(2,1)S(1)} %copy.41.v), custom_call_target="tpu_custom_call" | custom-call | flops 1073741824 | bytes 4194304 | tf_op jit(solution)/shard_map/pallas_call | solution.py:114
  121.2 1.0 copy-done.3
  122.2 0.3 collective-permute-start.7
  122.4 1.5 collective-permute-start.8
  123.9 1.8 collective-permute-start.9
  125.7 7.2 %shard_map.80 = f32[64,1024]{1,0:T(8,128)S(1)} custom-call(bf16[4,8,512,128]{3,2,1,0:T(8,128)(2,1)} %bitcast.78, bf16[8,256,512]{2,1,0:T(8,128)(2,1)S(1)} %copy-done.1, bf16[1024,1024]{1,0:T(8,128)(2,1)S(1)} %bitcast.71), custom_call_target="tpu_custom_call" | custom-call | flops 2147483648 | bytes 4194304 | tf_op jit(solution)/shard_map/pallas_call | solution.py:160
  132.8 0.0 copy-start.4
  132.8 1.0 copy.43
  133.8 1.1 reduce_sum.29
  134.9 0.1 copy.44
  135.1 0.1 reshape.73
  135.2 2.1 %collective-permute-done.7 = bf16[8,64,512]{2,1,0:T(8,128)(2,1)} collective-permute-done((bf16[8,64,512]{2,1,0:T(8,128)(2,1)}, bf16[8,64,512]{2,1,0:T(8,128)(2,1)}, u32[]{:S(2)}, u32[]{:S(2)}) %collective-permute-start.7) | collective-permute-done | bytes 524320 | tf_op jit(solution)/shard_map/ppermute | solution.py:222
  137.3 9.9 %collective-permute-done.8 = bf16[8,64,512]{2,1,0:T(8,128)(2,1)} collective-permute-done((bf16[8,64,512]{2,1,0:T(8,128)(2,1)}, bf16[8,64,512]{2,1,0:T(8,128)(2,1)}, u32[]{:S(2)}, u32[]{:S(2)}) %collective-permute-start.8) | collective-permute-done | bytes 524320 | tf_op jit(solution)/shard_map/ppermute | solution.py:222
  147.3 0.0 collective-permute-done.9
  147.3 1.9 multiply_reduce_fusion.mine
  149.1 11.8 %shard_map.78 = f32[8,512]{1,0:T(8,128)S(1)} custom-call(f32[8,512]{1,0:T(8,128)S(1)} %multiply_reduce_fusion.mine), custom_call_target="tpu_custom_call" | custom-call | tf_op jit(solution)/shard_map/pallas_call | solution.py:72
  160.9 2.7 %fusion.4 = bf16[8,512,64]{1,2,0:T(8,128)(2,1)} fusion(f32[8,64,512]{2,1,0:T(8,128)S(1)} %copy-done.7, f32[8,512]{1,0:T(8,128)S(1)} %shard_map.78, bf16[8,64,512]{2,1,0:T(8,128)(2,1)} %collective-permute-done.9, bf16[8,64,512]{2,1,0:T(8,128)(2,1)} %collective-permute-done.8, f32[8,64,512]{2,1,0:T(8,128)S(1)} %copy-done.4, ...), kind=kLoop, calls=%fused_computation.15 | loop fusion | flops 2359296 | bytes 4210688 | tf_op jit(solution)/shard_map/transpose | solution.py:263
  163.5 1.5 copy.42
  165.1 0.8 reshape.68.d_logits
  165.9 10.5 %shard_map.79 = (bf16[32768,128]{1,0:T(8,128)(2,1)}, f32[8,128]{1,0:T(8,128)S(1)}) custom-call(bf16[8,32768]{1,0:T(8,128)(2,1)S(1)} %reshape.68.d_logits, bf16[32768,128]{1,0:T(8,128)(2,1)} %bitcast.74, bf16[8,128]{1,0:T(8,128)(2,1)S(1)} %bitcast.72), custom_call_target="tpu_custom_call" | custom-call | tf_op jit(solution)/shard_map/pallas_call | solution.py:192
  176.4 1.2 shard_map.81.mine
  177.6 13.0 %shard_map.82 = f32[40,128]{1,0:T(8,128)S(1)} custom-call(f32[40,128]{1,0:T(8,128)S(1)} %shard_map.81.mine), custom_call_target="tpu_custom_call" | custom-call | tf_op jit(solution)/shard_map/pallas_call | solution.py:72
  190.6 0.6 slice_bitcast_fusion.2
  191.2 0.7 slice.21
  (22 shorter events, 0.1 us)
Async XLA Ops:
  7.2 1.2 copy-start
  7.2 104.5 %all-gather.3.cloned.1.call-start = ((), (), s32[]{:S(2)}) async-start(), calls=%async_computation | async-start | bytes 5242880 | tf_op jit(solution)/shard_map/all_gather | solution.py:228
  13.9 4.9 %copy-start.5 = (bf16[128,8]{0,1:T(8,128)(2,1)S(1)}, bf16[128,8]{0,1:T(8,128)(2,1)}, u32[]{:S(2)}) copy-start(bf16[128,8]{0,1:T(8,128)(2,1)} %param.6) | copy-start | bytes 6148
  15.3 49.1 %collective-permute-start = (bf16[2,16,64,64]{3,2,1,0:T(8,128)(2,1)}, bf16[2,16,64,64]{3,2,1,0:T(8,128)(2,1)}, u32[]{:S(2)}, u32[]{:S(2)}) collective-permute-start(bf16[2,16,64,64]{3,2,1,0:T(8,128)(2,1)} %get-tuple-element.38), channel_id=1, source_target_pairs={{0,1},{1,0},{2,3},{3,2},{4,5},{5,4},{6,7},{7,6},{8,9},{9,8},{10,11... | collective-permute-start | bytes 786440 | tf_op jit(solution)/shard_map/ppermute | solution.py:222
  16.8 47.6 %collective-permute-start.1 = (bf16[2,16,64,64]{3,2,1,0:T(8,128)(2,1)}, bf16[2,16,64,64]{3,2,1,0:T(8,128)(2,1)}, u32[]{:S(2)}, u32[]{:S(2)}) collective-permute-start(bf16[2,16,64,64]{3,2,1,0:T(8,128)(2,1)} %get-tuple-element.37), channel_id=1, source_target_pairs={{0,2},{1,3},{2,0},{3,1},{4,6},{5,7},{6,4},{7,5},{8,10},{9,11},{10,... | collective-permute-start | bytes 786440 | tf_op jit(solution)/shard_map/ppermute | solution.py:222
  17.3 47.1 %collective-permute-start.2 = (bf16[2,16,64,64]{3,2,1,0:T(8,128)(2,1)}, bf16[2,16,64,64]{3,2,1,0:T(8,128)(2,1)}, u32[]{:S(2)}, u32[]{:S(2)}) collective-permute-start(bf16[2,16,64,64]{3,2,1,0:T(8,128)(2,1)} %get-tuple-element.36), channel_id=1, source_target_pairs={{0,3},{1,2},{2,1},{3,0},{4,7},{5,6},{6,5},{7,4},{8,11},{9,10},{10,... | collective-permute-start | bytes 786440 | tf_op jit(solution)/shard_map/ppermute | solution.py:222
  31.0 33.4 %copy-start.8 = (bf16[2,16,64,64]{3,2,1,0:T(8,128)(2,1)S(1)}, bf16[2,16,64,64]{3,2,1,0:T(8,128)(2,1)}, u32[]{:S(2)}) copy-start(bf16[2,16,64,64]{3,2,1,0:T(8,128)(2,1)} %get-tuple-element.35) | copy-start | bytes 786436
  68.9 2.8 %copy-start.6 = (f32[512,64,8]{0,1,2:T(8,128)S(1)}, f32[512,64,8]{0,1,2:T(8,128)}, u32[]{:S(2)}) copy-start(f32[512,64,8]{0,1,2:T(8,128)} %copy.40) | copy-start | bytes 3145732
  71.7 31.8 %collective-permute-start.3 = (bf16[2,16,256,64]{2,3,1,0:T(8,128)(2,1)}, bf16[2,16,256,64]{2,3,1,0:T(8,128)(2,1)}, u32[]{:S(2)}, u32[]{:S(2)}) collective-permute-start(bf16[2,16,256,64]{2,3,1,0:T(8,128)(2,1)} %copy.37), channel_id=1, source_target_pairs={{0,16},{16,0},{1,17},{17,1},{2,18},{18,2},{3,19},{19,3},{4,20},{20... | collective-permute-start | bytes 3145736 | tf_op jit(solution)/shard_map/ppermute | solution.py:239
  72.9 15.2 %collective-permute-start.4 = (bf16[8,64,512]{2,1,0:T(8,128)(2,1)S(1)}, bf16[8,64,512]{2,1,0:T(8,128)(2,1)S(1)}, u32[]{:S(2)}, u32[]{:S(2)}) collective-permute-start(bf16[8,64,512]{2,1,0:T(8,128)(2,1)S(1)} %get-tuple-element.31), channel_id=1, source_target_pairs={{0,1},{1,0},{2,3},{3,2},{4,5},{5,4},{6,7},{7,6},{8,9},{9,8},{10,11... | collective-permute-start | bytes 1572872 | tf_op jit(solution)/shard_map/ppermute | solution.py:222
  75.4 25.4 %collective-permute-start.5 = (bf16[8,64,512]{2,1,0:T(8,128)(2,1)S(1)}, bf16[8,64,512]{2,1,0:T(8,128)(2,1)}, u32[]{:S(2)}, u32[]{:S(2)}) collective-permute-start(bf16[8,64,512]{2,1,0:T(8,128)(2,1)S(1)} %get-tuple-element.31), channel_id=1, source_target_pairs={{0,2},{1,3},{2,0},{3,1},{4,6},{5,7},{6,4},{7,5},{8,10},{9,11},{10,... | collective-permute-start | bytes 1572872 | tf_op jit(solution)/shard_map/ppermute | solution.py:222
  75.4 25.4 %collective-permute-start.6 = (bf16[8,64,512]{2,1,0:T(8,128)(2,1)S(1)}, bf16[8,64,512]{2,1,0:T(8,128)(2,1)}, u32[]{:S(2)}, u32[]{:S(2)}) collective-permute-start(bf16[8,64,512]{2,1,0:T(8,128)(2,1)S(1)} %get-tuple-element.31), channel_id=1, source_target_pairs={{0,3},{1,2},{2,1},{3,0},{4,7},{5,6},{6,5},{7,4},{8,11},{9,10},{10,... | collective-permute-start | bytes 1572872 | tf_op jit(solution)/shard_map/ppermute | solution.py:222
  107.8 1.9 copy-start.9
  114.6 11.1 %copy-start.1 = (bf16[8,256,512]{2,1,0:T(8,128)(2,1)S(1)}, bf16[8,256,512]{2,1,0:T(8,128)(2,1)}, u32[]{:S(2)}) copy-start(bf16[8,256,512]{2,1,0:T(8,128)(2,1)} %pad_maximum_fusion.1.p) | copy-start | bytes 6291460
  114.6 11.1 %copy-start.2 = (bf16[128,8,4,256]{3,1,2,0:T(8,128)(2,1)S(1)}, bf16[128,8,4,256]{3,1,2,0:T(8,128)(2,1)}, u32[]{:S(2)}) copy-start(bf16[128,8,4,256]{3,1,2,0:T(8,128)(2,1)} %copy.46) | copy-start | bytes 6291460
  121.2 1.0 copy-start.3
  122.2 15.2 %collective-permute-start.7 = (bf16[8,64,512]{2,1,0:T(8,128)(2,1)}, bf16[8,64,512]{2,1,0:T(8,128)(2,1)}, u32[]{:S(2)}, u32[]{:S(2)}) collective-permute-start(bf16[8,64,512]{2,1,0:T(8,128)(2,1)} %get-tuple-element.24), channel_id=1, source_target_pairs={{0,1},{1,0},{2,3},{3,2},{4,5},{5,4},{6,7},{7,6},{8,9},{9,8},{10,11... | collective-permute-start | bytes 1572872 | tf_op jit(solution)/shard_map/ppermute | solution.py:222
  122.4 24.8 %collective-permute-start.8 = (bf16[8,64,512]{2,1,0:T(8,128)(2,1)}, bf16[8,64,512]{2,1,0:T(8,128)(2,1)}, u32[]{:S(2)}, u32[]{:S(2)}) collective-permute-start(bf16[8,64,512]{2,1,0:T(8,128)(2,1)} %get-tuple-element.25), channel_id=1, source_target_pairs={{0,2},{1,3},{2,0},{3,1},{4,6},{5,7},{6,4},{7,5},{8,10},{9,11},{10,... | collective-permute-start | bytes 1572872 | tf_op jit(solution)/shard_map/ppermute | solution.py:222
  123.9 23.4 %collective-permute-start.9 = (bf16[8,64,512]{2,1,0:T(8,128)(2,1)}, bf16[8,64,512]{2,1,0:T(8,128)(2,1)}, u32[]{:S(2)}, u32[]{:S(2)}) collective-permute-start(bf16[8,64,512]{2,1,0:T(8,128)(2,1)} %get-tuple-element.26), channel_id=1, source_target_pairs={{0,3},{1,2},{2,1},{3,0},{4,7},{5,6},{6,5},{7,4},{8,11},{9,10},{10,... | collective-permute-start | bytes 1572872 | tf_op jit(solution)/shard_map/ppermute | solution.py:222
  125.7 21.6 %copy-start.7 = (f32[8,64,512]{2,1,0:T(8,128)S(1)}, f32[8,64,512]{2,1,0:T(8,128)}, u32[]{:S(2)}) copy-start(f32[8,64,512]{2,1,0:T(8,128)} %get-tuple-element.20) | copy-start | bytes 3145732
  132.8 14.4 %copy-start.4 = (f32[8,64,512]{2,1,0:T(8,128)S(1)}, f32[8,64,512]{2,1,0:T(8,128)}, u32[]{:S(2)}) copy-start(f32[8,64,512]{2,1,0:T(8,128)} %copy-done.3) | copy-start | bytes 3145732
Sparse Core Ops, SparseCore 0:
  10.0 89.2 all-gather.2

commit v3 on v2

--- a/solution.py
+++ b/solution.py
@@ -252,7 +252,7 @@
     v = v.transpose(3, 2, 0, 1, 4).reshape(heads, group * tokens, blocks // group * lanes)
     f = everyone.transpose(1, 3, 0, 2).reshape(strands * width, blocks * tokens)
 
-    g, v, f, probs, probs_low = lax.optimization_barrier((g, v, f, probs, probs_low))
+    g, v, probs = lax.optimization_barrier((g, v, probs))
     d_probs, *d_others = d_probs_of(g, v, group)
     for d, other in enumerate(d_others, 1):
         d_probs += swap(other, d).astype(jnp.float32)

time: 200 us -> 188 us (0.940)
  waiting for transfers between devices: 32.7 us -> 28 us
  other arithmetic: 16.8 us -> 13.6 us
  local copies, waits for them, and re-layouts: 30.6 us -> 28.2 us
    ppermute x9, waiting for transfers between devices: 32.7 us -> 20.9 us  [swap(): return lax.ppermute(x, 'col', [(c, c ^ d) for c in range(blocks)])]
    all_gather x1, waiting for transfers between devices: 0.01 us -> 7.12 us  [on_device(): g = lax.all_gather(g, 'col', axis=0, axis_index_groups=groups)]
    unnamed x22 -> x20, local copies, waits for them, and re-layouts: 5.32 us -> 4 us
  transfers between devices with their start and end apart: 11 -> 11, of which waited for: 4 -> 3; matrix products, arithmetic and copies ran while one was open for 23% -> 23% of each run, Pallas kernels for 19% -> 23%
where the time goes in v3:
time: 188 us
  Pallas kernels  80.2 us (43%)
  local copies, waits for them, and re-layouts  28.2 us (15%)
  waiting for transfers between devices  28 us (15%)
  between operations  14.4 us (8%)
  other arithmetic  13.6 us (7%)
  matrix products  12.6 us (7%)
  starting transfers between devices  10.6 us (6%)
    pallas_call x4, Pallas kernels, exchange(): pl.pallas_call(functools.partial(exchange_kernel, axes, combine), out_sha...  55.9 us
    ppermute x9, waiting for transfers between devices, swap(): return lax.ppermute(x, 'col', [(c, c ^ d) for c in range(blocks)])  20.9 us
    dot_general x1, matrix products, on_device(): jnp.einsum('ijk,kh->hji', pair, pair_weight, preferred_element_type=jnp.f...  10.6 us
    ppermute x9, starting transfers between devices, swap(): return lax.ppermute(x, 'col', [(c, c ^ d) for c in range(blocks)])  10.5 us
    pallas_call x1, Pallas kernels, pair_gradients(): pl.pallas_call(pair_kernel, grid=(cells // block,), in_specs=[pl.BlockSpe...  10.5 us
    pallas_call x1, Pallas kernels, value_weight_of(): pl.pallas_call(functools.partial(value_kernel, heads, strands), grid=(ste...  7.18 us
    all_gather x1, waiting for transfers between devices, on_device(): g = lax.all_gather(g, 'col', axis=0, axis_index_groups=groups)  7.12 us
    pallas_call x1, Pallas kernels, d_probs_of(): pl.pallas_call(functools.partial(d_probs_kernel, heads, tokens // group),...  6.64 us
  transfers between devices with their start and end apart: 11, of which 3 were waited for; matrix products, arithmetic and copies ran while one was open for 23% of the time, Pallas kernels for 23%

profile of v3, /device:TPU:12, one launch (start us, length us, event | category | flops | bytes accessed | tf_op | source)
XLA Modules:
  0.0 187.6 jit_solution(334558089408591423)
XLA Ops:
  7.2 0.0 copy-start
  7.2 0.0 all-gather.3.cloned.1.call-start
  7.2 1.2 copy-done
  8.4 0.1 copy_bitcast_fusion
  8.5 1.3 copy.34
  9.8 0.0 all-gather.3.cloned.1.call-update
  9.8 3.9 %copy.35 = bf16[128,64,64]{2,1,0:T(8,128)(2,1)S(1)} copy(bf16[128,64,64]{0,2,1:T(8,128)(2,1)} %param.7) | data formatting | bytes 2097152 | tf_op jit(solution)/shard_map/optimization_barrier | solution.py:227
  13.8 0.0 copy-start.3
  13.8 1.4 dynamic-slice_bitcast_fusion.3
  15.2 1.5 collective-permute-start
  16.7 0.5 collective-permute-start.1
  17.2 1.5 collective-permute-start.2
  18.7 10.6 %fusion.5 = f32[512,64,8]{1,2,0:T(8,128)S(1)} fusion(bf16[512,64,128]{2,1,0:T(8,128)(2,1)} %param.5, bf16[128,8]{0,1:T(8,128)(2,1)S(1)} %copy-done.3), kind=kOutput, calls=%fused_computation.26 | convolution fusion | flops 67108864 | bytes 9439232 | tf_op jit(solution)/shard_map/ijk,kh->hji/dot_general | solution.py:242
  29.2 1.8 copy.39
  31.0 0.0 collective-permute-done
  31.0 10.6 %collective-permute-done.1 = bf16[2,16,64,64]{3,2,1,0:T(8,128)(2,1)} collective-permute-done((bf16[2,16,64,64]{3,2,1,0:T(8,128)(2,1)}, bf16[2,16,64,64]{3,2,1,0:T(8,128)(2,1)}, u32[]{:S(2)}, u32[]{:S(2)}) %collective-permute-start.1) | collective-permute-done | bytes 262176 | tf_op jit(solution)/shard_map/ppermute | solution.py:222
  41.6 4.6 %pad_maximum_fusion = (bf16[2,16,256,64]{3,2,1,0:T(8,128)(2,1)}, bf16[1,2,16,256,64]{4,3,2,1,0:T(8,128)(2,1)}) fusion(bf16[2,16,64,64]{3,2,1,0:T(8,128)(2,1)} %collective-permute-done.2, bf16[2,16,64,64]{3,2,1,0:T(8,128)(2,1)} %collective-permute-done.1, bf16[2,16,64,64]{3,2,1,0:T(8,128)(2,1)} %collective-permute-done, ...), kind=kLoop, calls=%fused_computation.1 | loop fusion | flops 4194304 | bytes 3145728 | tf_op jit(solution)/shard_map/concatenate | solution.py:233
  46.2 2.0 %copy.37 = bf16[2,16,256,64]{2,3,1,0:T(8,128)(2,1)S(1)} copy(bf16[2,16,256,64]{3,2,1,0:T(8,128)(2,1)} %get-tuple-element.29) | data formatting | bytes 2097152 | tf_op jit(solution)/shard_map/concatenate | solution.py:233
  48.2 0.1 collective-permute-start.3
  48.3 0.1 bitcast_reduce_fusion
  48.4 0.2 fusion.1
  48.6 30.2 %shard_map.76 = f32[2,8,512]{2,1,0:T(8,128)S(1)} custom-call(f32[2,8,512]{2,1,0:T(8,128)S(1)} %pad_maximum_fusion.2.mine), custom_call_target="tpu_custom_call" | custom-call | tf_op jit(solution)/shard_map/pallas_call | solution.py:72
  78.8 1.4 fusion.8
  80.2 0.6 collective-permute-start.7
  80.8 1.7 collective-permute-start.8
  82.5 1.2 collective-permute-start.9
  83.7 2.7 %copy.36 = bf16[1,2,16,256,64]{3,2,1,0,4:T(8,128)(2,1)S(1)} copy(bf16[1,2,16,256,64]{4,3,2,1,0:T(8,128)(2,1)} %get-tuple-element.30) | data formatting | bytes 2097152 | tf_op jit(solution)/shard_map/jit(dynamic_update_index_in_dim)/broadcast_in_dim | solution.py:240
  86.4 0.3 broadcast_in_dim.12
  86.7 0.1 constant_dynamic-update-slice_fusion
  86.8 1.9 copy_dynamic-update-slice_fusion
  88.7 0.0 copy-start.8
  88.7 1.3 copy.45
  90.0 0.1 copy-done.4
  90.0 2.1 %convolution_convert_fusion = bf16[16384,64]{0,1:T(8,128)(2,1)} fusion(bf16[16384,64]{0,1:T(8,128)(2,1)S(1)} %bitcast.80, bf16[64,64]{1,0:T(8,128)(2,1)S(1)} %copy-done.8), kind=kOutput, calls=%fused_computation | convolution fusion | flops 135266304 | bytes 4202496 | tf_op jit(solution)/shard_map/dot_general | solution.py:250
  92.1 7.1 %all-gather.3.cloned.1.call-done = bf16[32,512,128]{2,1,0:T(8,128)(2,1)} async-done(((bf16[8,512,128]{2,1,0:T(8,128)(2,1)}), bf16[32,512,128]{2,1,0:T(8,128)(2,1)}) %all-gather.3.cloned.1.call-update) | async-done | bytes 4194320 | tf_op jit(solution)/shard_map/all_gather | solution.py:228
  99.2 2.9 %copy.40.v = bf16[8,256,512]{2,1,0:T(8,128)(2,1)S(1)} copy(bf16[8,256,512]{1,2,0:T(8,128)(2,1)} %bitcast.79) | data formatting | bytes 4194304 | tf_op jit(solution)/shard_map/optimization_barrier | solution.py:255
  102.1 6.6 %shard_map.77 = (f32[8,64,512]{2,1,0:T(8,128)S(1)}, bf16[8,64,512]{2,1,0:T(8,128)(2,1)}, bf16[8,64,512]{2,1,0:T(8,128)(2,1)}, bf16[8,64,512]{2,1,0:T(8,128)(2,1)}) custom-call(bf16[4,8,512,128]{3,2,1,0:T(8,128)(2,1)} %bitcast.77, bf16[8,256,512]{2,1,0:T(8,128)(2,1)S(1)} %copy.40.v), custom_call_target="tpu_custom_call" | custom-call | flops 1073741824 | bytes 4194304 | tf_op jit(solution)/shard_map/pallas_call | solution.py:114
  108.7 1.0 copy-done.1
  109.7 1.5 collective-permute-start.4
  111.2 0.6 collective-permute-start.5
  111.7 0.0 collective-permute-done.7
  111.7 1.5 collective-permute-start.6
  113.2 0.0 collective-permute-done.9
  113.2 1.7 pad_maximum_fusion.1.p
  114.9 1.1 copy.42
  116.0 0.5 copy.46
  116.5 7.2 %shard_map.80 = f32[64,1024]{1,0:T(8,128)S(1)} custom-call(bf16[4,8,512,128]{3,2,1,0:T(8,128)(2,1)} %bitcast.78, bf16[8,256,512]{2,1,0:T(8,128)(2,1)S(1)} %pad_maximum_fusion.1.p, bf16[1024,1024]{1,0:T(8,128)(2,1)S(1)} %bitcast.71), custom_call_target="tpu_custom_call" | custom-call | flops 2147483648 | bytes 4194304 | tf_op jit(solution)/shard_map/pallas_call | solution.py:160
  123.7 0.0 copy-start.2
  123.7 1.0 copy.43
  124.7 1.1 reduce_sum.29
  125.8 0.1 copy.44
  125.9 0.1 reshape.73
  126.1 10.3 %collective-permute-done.5 = bf16[8,64,512]{2,1,0:T(8,128)(2,1)} collective-permute-done((bf16[8,64,512]{2,1,0:T(8,128)(2,1)}, bf16[8,64,512]{2,1,0:T(8,128)(2,1)}, u32[]{:S(2)}, u32[]{:S(2)}) %collective-permute-start.5) | collective-permute-done | bytes 524320 | tf_op jit(solution)/shard_map/ppermute | solution.py:222
  136.3 0.0 collective-permute-done.6
  136.3 1.9 multiply_reduce_fusion.mine
  138.2 12.0 %shard_map.78 = f32[8,512]{1,0:T(8,128)S(1)} custom-call(f32[8,512]{1,0:T(8,128)S(1)} %multiply_reduce_fusion.mine), custom_call_target="tpu_custom_call" | custom-call | tf_op jit(solution)/shard_map/pallas_call | solution.py:72
  150.3 2.7 %fusion.4 = bf16[8,512,64]{1,2,0:T(8,128)(2,1)} fusion(f32[8,64,512]{2,1,0:T(8,128)S(1)} %copy-done.7, f32[8,512]{1,0:T(8,128)S(1)} %shard_map.78, bf16[8,64,512]{2,1,0:T(8,128)(2,1)} %collective-permute-done.6, bf16[8,64,512]{2,1,0:T(8,128)(2,1)} %collective-permute-done.5, f32[8,64,512]{2,1,0:T(8,128)S(1)} %copy-done.2, ...), kind=kLoop, calls=%fused_computation.15 | loop fusion | flops 2359296 | bytes 4210688 | tf_op jit(solution)/shard_map/transpose | solution.py:263
  152.9 1.5 copy.41
  154.4 0.8 reshape.66.d_logits
  155.3 10.5 %shard_map.79 = (bf16[32768,128]{1,0:T(8,128)(2,1)}, f32[8,128]{1,0:T(8,128)S(1)}) custom-call(bf16[8,32768]{1,0:T(8,128)(2,1)S(1)} %reshape.66.d_logits, bf16[32768,128]{1,0:T(8,128)(2,1)} %bitcast.74, bf16[8,128]{1,0:T(8,128)(2,1)S(1)} %bitcast.72), custom_call_target="tpu_custom_call" | custom-call | tf_op jit(solution)/shard_map/pallas_call | solution.py:192
  165.7 1.2 shard_map.81.mine
  167.0 12.5 %shard_map.82 = f32[40,128]{1,0:T(8,128)S(1)} custom-call(f32[40,128]{1,0:T(8,128)S(1)} %shard_map.81.mine), custom_call_target="tpu_custom_call" | custom-call | tf_op jit(solution)/shard_map/pallas_call | solution.py:72
  179.5 0.6 slice_bitcast_fusion.2
  180.1 0.7 slice.21
  (20 shorter events, 0.1 us)
Async XLA Ops:
  7.2 1.2 copy-start
  7.2 92.0 %all-gather.3.cloned.1.call-start = ((), (), s32[]{:S(2)}) async-start(), calls=%async_computation | async-start | bytes 5242880 | tf_op jit(solution)/shard_map/all_gather | solution.py:228
  13.8 4.9 %copy-start.3 = (bf16[128,8]{0,1:T(8,128)(2,1)S(1)}, bf16[128,8]{0,1:T(8,128)(2,1)}, u32[]{:S(2)}) copy-start(bf16[128,8]{0,1:T(8,128)(2,1)} %param.6) | copy-start | bytes 6148
  15.2 15.8 %collective-permute-start = (bf16[2,16,64,64]{3,2,1,0:T(8,128)(2,1)}, bf16[2,16,64,64]{3,2,1,0:T(8,128)(2,1)}, u32[]{:S(2)}, u32[]{:S(2)}) collective-permute-start(bf16[2,16,64,64]{3,2,1,0:T(8,128)(2,1)} %get-tuple-element.34), channel_id=1, source_target_pairs={{0,1},{1,0},{2,3},{3,2},{4,5},{5,4},{6,7},{7,6},{8,9},{9,8},{10,11... | collective-permute-start | bytes 786440 | tf_op jit(solution)/shard_map/ppermute | solution.py:222
  16.7 24.9 %collective-permute-start.1 = (bf16[2,16,64,64]{3,2,1,0:T(8,128)(2,1)}, bf16[2,16,64,64]{3,2,1,0:T(8,128)(2,1)}, u32[]{:S(2)}, u32[]{:S(2)}) collective-permute-start(bf16[2,16,64,64]{3,2,1,0:T(8,128)(2,1)} %get-tuple-element.33), channel_id=1, source_target_pairs={{0,2},{1,3},{2,0},{3,1},{4,6},{5,7},{6,4},{7,5},{8,10},{9,11},{10,... | collective-permute-start | bytes 786440 | tf_op jit(solution)/shard_map/ppermute | solution.py:222
  17.2 24.4 %collective-permute-start.2 = (bf16[2,16,64,64]{3,2,1,0:T(8,128)(2,1)}, bf16[2,16,64,64]{3,2,1,0:T(8,128)(2,1)}, u32[]{:S(2)}, u32[]{:S(2)}) collective-permute-start(bf16[2,16,64,64]{3,2,1,0:T(8,128)(2,1)} %get-tuple-element.32), channel_id=1, source_target_pairs={{0,3},{1,2},{2,1},{3,0},{4,7},{5,6},{6,5},{7,4},{8,11},{9,10},{10,... | collective-permute-start | bytes 786440 | tf_op jit(solution)/shard_map/ppermute | solution.py:222
  46.2 2.1 %copy-start.6 = (f32[512,64,8]{0,1,2:T(8,128)S(1)}, f32[512,64,8]{0,1,2:T(8,128)}, u32[]{:S(2)}) copy-start(f32[512,64,8]{0,1,2:T(8,128)} %copy.39) | copy-start | bytes 3145732
  48.2 38.6 %collective-permute-start.3 = (bf16[2,16,256,64]{2,3,1,0:T(8,128)(2,1)S(1)}, bf16[2,16,256,64]{2,3,1,0:T(8,128)(2,1)}, u32[]{:S(2)}, u32[]{:S(2)}) collective-permute-start(bf16[2,16,256,64]{2,3,1,0:T(8,128)(2,1)S(1)} %copy.37), channel_id=1, source_target_pairs={{0,16},{16,0},{1,17},{17,1},{2,18},{18,2},{3,19},{19,3},{4,20},{20... | collective-permute-start | bytes 3145736 | tf_op jit(solution)/shard_map/ppermute | solution.py:239
  80.2 31.5 %collective-permute-start.7 = (bf16[8,64,512]{2,1,0:T(8,128)(2,1)}, bf16[8,64,512]{2,1,0:T(8,128)(2,1)}, u32[]{:S(2)}, u32[]{:S(2)}) collective-permute-start(bf16[8,64,512]{2,1,0:T(8,128)(2,1)} %get-tuple-element.27), channel_id=1, source_target_pairs={{0,1},{1,0},{2,3},{3,2},{4,5},{5,4},{6,7},{7,6},{8,9},{9,8},{10,11... | collective-permute-start | bytes 1572872 | tf_op jit(solution)/shard_map/ppermute | solution.py:222
  80.8 32.4 %collective-permute-start.8 = (bf16[8,64,512]{2,1,0:T(8,128)(2,1)}, bf16[8,64,512]{2,1,0:T(8,128)(2,1)}, u32[]{:S(2)}, u32[]{:S(2)}) collective-permute-start(bf16[8,64,512]{2,1,0:T(8,128)(2,1)} %get-tuple-element.27), channel_id=1, source_target_pairs={{0,2},{1,3},{2,0},{3,1},{4,6},{5,7},{6,4},{7,5},{8,10},{9,11},{10,... | collective-permute-start | bytes 1572872 | tf_op jit(solution)/shard_map/ppermute | solution.py:222
  82.5 30.7 %collective-permute-start.9 = (bf16[8,64,512]{2,1,0:T(8,128)(2,1)}, bf16[8,64,512]{2,1,0:T(8,128)(2,1)}, u32[]{:S(2)}, u32[]{:S(2)}) collective-permute-start(bf16[8,64,512]{2,1,0:T(8,128)(2,1)} %get-tuple-element.27), channel_id=1, source_target_pairs={{0,3},{1,2},{2,1},{3,0},{4,7},{5,6},{6,5},{7,4},{8,11},{9,10},{10,... | collective-permute-start | bytes 1572872 | tf_op jit(solution)/shard_map/ppermute | solution.py:222
  88.7 1.4 copy-start.4
  88.7 1.3 copy-start.8
  108.7 1.0 copy-start.1
  109.7 16.4 %collective-permute-start.4 = (bf16[8,64,512]{2,1,0:T(8,128)(2,1)}, bf16[8,64,512]{2,1,0:T(8,128)(2,1)}, u32[]{:S(2)}, u32[]{:S(2)}) collective-permute-start(bf16[8,64,512]{2,1,0:T(8,128)(2,1)} %get-tuple-element.22), channel_id=1, source_target_pairs={{0,1},{1,0},{2,3},{3,2},{4,5},{5,4},{6,7},{7,6},{8,9},{9,8},{10,11... | collective-permute-start | bytes 1572872 | tf_op jit(solution)/shard_map/ppermute | solution.py:222
  111.2 25.2 %collective-permute-start.5 = (bf16[8,64,512]{2,1,0:T(8,128)(2,1)}, bf16[8,64,512]{2,1,0:T(8,128)(2,1)}, u32[]{:S(2)}, u32[]{:S(2)}) collective-permute-start(bf16[8,64,512]{2,1,0:T(8,128)(2,1)} %get-tuple-element.23), channel_id=1, source_target_pairs={{0,2},{1,3},{2,0},{3,1},{4,6},{5,7},{6,4},{7,5},{8,10},{9,11},{10,... | collective-permute-start | bytes 1572872 | tf_op jit(solution)/shard_map/ppermute | solution.py:222
  111.7 3.1 %copy-start.5 = (bf16[2,2,16,256,64]{3,2,1,0,4:T(8,128)(2,1)S(1)}, bf16[2,2,16,256,64]{3,2,1,0,4:T(8,128)(2,1)}, u32[]{:S(2)}) copy-start(bf16[2,2,16,256,64]{3,2,1,0,4:T(8,128)(2,1)} %copy-done.4) | copy-start | bytes 6291460
  111.7 24.6 %collective-permute-start.6 = (bf16[8,64,512]{2,1,0:T(8,128)(2,1)}, bf16[8,64,512]{2,1,0:T(8,128)(2,1)}, u32[]{:S(2)}, u32[]{:S(2)}) collective-permute-start(bf16[8,64,512]{2,1,0:T(8,128)(2,1)} %get-tuple-element.24), channel_id=1, source_target_pairs={{0,3},{1,2},{2,1},{3,0},{4,7},{5,6},{6,5},{7,4},{8,11},{9,10},{10,... | collective-permute-start | bytes 1572872 | tf_op jit(solution)/shard_map/ppermute | solution.py:222
  116.5 19.9 %copy-start.7 = (f32[8,64,512]{2,1,0:T(8,128)S(1)}, f32[8,64,512]{2,1,0:T(8,128)}, u32[]{:S(2)}) copy-start(f32[8,64,512]{2,1,0:T(8,128)} %get-tuple-element.18) | copy-start | bytes 3145732
  123.7 12.7 %copy-start.2 = (f32[8,64,512]{2,1,0:T(8,128)S(1)}, f32[8,64,512]{2,1,0:T(8,128)}, u32[]{:S(2)}) copy-start(f32[8,64,512]{2,1,0:T(8,128)} %copy-done.1) | copy-start | bytes 3145732
Sparse Core Ops, SparseCore 0:
  9.9 89.2 all-gather.2
